TPU v7x, 256 devices: a whole 4x4x8 slice. The times are simulated.
256 devices in a mesh: slab: 64 (over z_lo, y, x, core), energy: 4 (over z_hi).
Axes of the slice: x: 4, y: 4, z: 8 (z_hi: 4, z_lo: 2; z = z_hi * 2 + z_lo), core: 2. Of those that a mesh axis runs over, the one named last changes fastest.
Arguments:
- green_blocks: float32 [512, 4, 2, 2, 128, 128], P('slab', 'energy'), may hold values from -1.1 to 1.1
- couplings: float32 [512, 128, 128], P('slab'), may hold values from -1.1 to 1.1
- green_cotangent: float32 [512, 4, 2, 2, 128, 128], P('slab', 'energy'), may hold values from -0.6 to 0.6
Outputs:
- onsite_grad: float32 [512, 128, 128], P('slab', 'energy')
- coupling_grad: float32 [512, 128, 128], P('slab', 'energy')
All inputs are finite; a program needn't handle non-finite values.
Results may differ from a plain program's by a relative error of at most 0.0003.
Values sent between devices are 32-bit elements; how exact they have to be, the bound alone decides.
A program may use at most 128 MiB of HBM per device.

v0:
```python
import jax
import jax.numpy as jnp
from jax import lax
from jax.sharding import PartitionSpec as P


def passed_along(array, axis, by):
    size = lax.axis_size(axis)
    pairs = [(i, i + by) for i in range(size) if 0 <= i + by < size]
    return lax.ppermute(array, axis, pairs)


def matprod(left, right):
    return jnp.matmul(left, right, precision=lax.Precision.HIGHEST)


def complex_prod(left, right):
    left_re = left[..., 0, :, :]
    left_im = left[..., 1, :, :]
    right_re = right[..., 0, :, :]
    right_im = right[..., 1, :, :]
    return jnp.stack(
        [
            matprod(left_re, right_re) - matprod(left_im, right_im),
            matprod(left_re, right_im) + matprod(left_im, right_re),
        ],
        axis=-3,
    )


def real_left(matrix, right):
    return jnp.stack(
        [matprod(matrix, right[..., 0, :, :]), matprod(matrix, right[..., 1, :, :])], axis=-3
    )


def real_right(left, matrix):
    return jnp.stack(
        [matprod(left[..., 0, :, :], matrix), matprod(left[..., 1, :, :], matrix)], axis=-3
    )


def flipped(value):
    return jnp.swapaxes(value, -1, -2)


def sandwich(outer, inner):
    return complex_prod(complex_prod(outer, inner), flipped(outer))


def on_device(green_blocks, couplings, green_cotangent):
    first_next = passed_along(green_blocks[0], "slab", -1)
    green_next = jnp.concatenate([green_blocks[1:], first_next[None]], axis=0)
    coupling_wide = couplings[:, None, None]
    linkage = real_left(coupling_wide, flipped(green_next))
    order = green_blocks.shape[-1]
    zeros = jnp.zeros(green_blocks.shape[1:], jnp.float32)
    unit = jnp.eye(order, dtype=jnp.float32)
    identity_block = jnp.broadcast_to(jnp.stack([unit, jnp.zeros_like(unit)], axis=0), zeros.shape)

    def fold_slab(carried, inputs):
        adjoint_acc, product_acc = carried
        cotangent, link_now = inputs
        return (
            (cotangent + sandwich(link_now, adjoint_acc), complex_prod(link_now, product_acc)),
            None,
        )

    (offset_map, product_map), _ = lax.scan(
        fold_slab, (zeros, identity_block), (green_cotangent, linkage), reverse=True
    )

    def relay(turn_index, incoming_now):
        return passed_along(offset_map + sandwich(product_map, incoming_now), "slab", -1)

    incoming = lax.fori_loop(0, lax.axis_size("slab") - 1, relay, zeros)

    def expand_slab(adjoint_next, inputs):
        cotangent, link_now = inputs
        adjoint_now = cotangent + sandwich(link_now, adjoint_next)
        return (adjoint_now, adjoint_now)

    _, adjoints = lax.scan(expand_slab, incoming, (green_cotangent, linkage), reverse=True)
    green_flip = flipped(green_blocks)
    weights = complex_prod(complex_prod(green_flip, adjoints), green_flip)
    onsite = jnp.sum(weights[..., 0, :, :], axis=(1, 2))
    weight_first = passed_along(weights[0], "slab", -1)
    weight_next = jnp.concatenate([weights[1:], weight_first[None]], axis=0)
    forward_part = complex_prod(real_right(green_blocks, coupling_wide), flipped(weight_next))
    backward_part = complex_prod(real_right(green_flip, coupling_wide), weight_next)
    coupling = jnp.sum((forward_part + backward_part)[..., 0, :, :], axis=(1, 2))
    onsite_part, coupling_part = (
        lax.psum_scatter(onsite, "energy", scatter_dimension=1, tiled=True),
        lax.psum_scatter(coupling, "energy", scatter_dimension=1, tiled=True),
    )
    return (onsite_part, coupling_part)


def solution(mesh):
    in_specs = (
        P("slab", "energy", None, None, None, None),
        P("slab", None, None),
        P("slab", "energy", None, None, None, None),
    )
    out_specs = (P("slab", "energy", None), P("slab", "energy", None))
    return jax.shard_map(
        on_device, mesh=mesh, in_specs=in_specs, out_specs=out_specs, check_vma=False
    )
```

profile of v0, /device:TPU:1, one launch (start us, length us, event | category | flops | bytes accessed | tf_op | source)
XLA Modules:
  0.0 1141.6 jit_solution(2742163920539372216)
XLA Ops:
  30.8 59.0 %while.45 = (s32[]{:T(128)}, f32[1,2,2,128,128]{4,3,1,2,0:T(8,128)}, f32[1,2,2,128,128]{4,3,1,2,0:T(8,128)S(1)}, f32[8,1,2,2,128,128]{5,4,2,3,1,0:T(8,128)}, f32...) while((s32[]{:T(128)}, f32[1,2,2,128,128]{4,3,1,2,0:T(8,128)}, ...), condition=%wide.region_1.2_spmd.clone, body=%wide.region_0.1_spmd.clone.sunk | while | flops 604438528 | bytes 8126579 | solution.py:69
  89.8 738.9 %while.43 = (s32[]{:T(128)}, f32[1,2,2,128,128]{4,3,1,2,0:T(8,128)S(1)}, f32[1,2,2,128,128]{4,3,1,2,0:T(8,128)S(1)}, f32[1,2,2,128,128]{4,3,1,2,0:T(8,128)}, s32[]{:T(128)}) while((s32[]{:T(128)}, f32[1,2,2,128,128]{4,3,1,2,0:T(8,128)S(1)}, f32[1,2,2,128,128]{4,3,1,2,0:T(8,128)S(1)}, f32[1,2,2,128,128]{4,3,1,2,0:T(8,128)}, s32[]{:T(128)}) %tuple.99), condition=%wide.region_3.4_spmd, body=%wide.region_2.3_spmd.sunk | while | flops 402915328 | bytes 7078017 | solution.py:76
  235.5 7.9 collective-permute-done
  247.7 7.9 collective-permute-done
  259.9 7.9 collective-permute-done
  272.1 7.9 collective-permute-done
  284.3 7.9 collective-permute-done
  296.5 7.9 collective-permute-done
  308.7 7.9 collective-permute-done
  320.9 7.9 collective-permute-done
  333.1 7.9 collective-permute-done
  357.5 7.9 collective-permute-done
  369.7 7.9 collective-permute-done
  381.8 7.9 collective-permute-done
  394.0 7.9 collective-permute-done
  418.4 7.9 collective-permute-done
  430.6 7.9 collective-permute-done
  442.8 7.9 collective-permute-done
  455.0 7.9 collective-permute-done
  479.4 7.9 collective-permute-done
  491.6 7.9 collective-permute-done
  503.8 7.9 collective-permute-done
  516.0 7.9 collective-permute-done
  528.2 7.9 collective-permute-done
  540.4 7.9 collective-permute-done
  552.6 7.9 collective-permute-done
  564.8 7.9 collective-permute-done
  589.1 7.9 collective-permute-done
  601.3 7.9 collective-permute-done
  613.5 7.9 collective-permute-done
  625.7 7.9 collective-permute-done
  650.1 7.9 collective-permute-done
  662.3 7.9 collective-permute-done
  674.5 7.9 collective-permute-done
  686.7 7.9 collective-permute-done
  711.1 7.9 collective-permute-done
  723.3 7.9 collective-permute-done
  735.5 7.9 collective-permute-done
  747.7 7.9 collective-permute-done
  759.9 7.9 collective-permute-done
  772.0 7.9 collective-permute-done
  784.2 7.9 collective-permute-done
  796.4 7.9 collective-permute-done
  820.8 7.9 collective-permute-done
  830.3 52.4 %while.44 = (s32[]{:T(128)}, f32[1,2,2,128,128]{4,3,1,2,0:T(8,128)S(1)}, f32[8,1,2,2,128,128]{4,5,2,0,3,1:T(8,128)}, f32[8,1,2,2,128,128]{5,4,2,3,1,0:T(8,128)},...) while((s32[]{:T(128)}, f32[1,2,2,128,128]{4,3,1,2,0:T(8,128)S(1)}, ...), condition=%wide.region_5.6_spmd, body=%wide.region_4.5_spmd.sunk | while | flops 403046400 | bytes 7077993 | solution.py:83
  899.1 13.0 %fusion.104 = (f32[8,128,128]{2,1,0:T(8,128)}, f32[8,2,128,128]{3,2,1,0:T(8,128)S(1)}) fusion(f32[8,2,128,128]{3,2,1,0:T(8,128)S(1)} %fusion.84, f32[8,2,128,128]{3,2,1,0:T(8,128)S(1)} %convolution_add_fusion.10, f32[8,1,2,2,128,128]{5,4,2,0,3,1:T(8,128)S(1)} %bitcast.403), kind=kOutput, calls=%fused_computation.168 | convolution fusion | flops 403046400 | bytes 4718592 | tf_op jit(solution)/shard_map/dot_general | solution.py:14
  938.3 167.1 %reduce-scatter.3.cloned.1.call-done = f32[8,32,128]{2,1,0:T(8,128)} async-done(((f32[8,128,128]{2,1,0:T(8,128)}), f32[8,32,128]{2,1,0:T(8,128)}) %reduce-scatter.3.cloned.1.call-update) | async-done | bytes 131088 | tf_op jit(solution)/shard_map/reduce_scatter | solution.py:93
  1105.4 29.2 %reduce-scatter.5.cloned.1.call-done = f32[8,32,128]{2,1,0:T(8,128)} async-done(((f32[8,128,128]{2,1,0:T(8,128)}), f32[8,32,128]{2,1,0:T(8,128)}) %reduce-scatter.5.cloned.1.call-update) | async-done | bytes 131088 | tf_op jit(solution)/shard_map/reduce_scatter | solution.py:94
  (1129 shorter events, 579.5 us)
Async XLA Ops:
  7.2 1098.2 %reduce-scatter.3.cloned.1.call-start = ((), (), s32[]{:S(2)}) async-start(), calls=%async_computation.2 | async-start | bytes 655360 | tf_op jit(solution)/shard_map/reduce_scatter | solution.py:93
  8.2 15.8 %collective-permute-start.1 = (f32[1,2,2,128,128]{4,3,1,2,0:T(8,128)S(1)}, f32[1,2,2,128,128]{4,3,1,2,0:T(8,128)S(1)}, u32[]{:S(2)}, u32[]{:S(2)}) collective-permute-start(f32[1,2,2,128,128]{4,3,1,2,0:T(8,128)S(1)} %copy_bitcast_fusion), channel_id=1, source_target_pairs={{4,0},{8,4},{12,8},{16,12},{20,16},{24,20},{28,24},{32,28},{36,32}... | collective-permute-start | bytes 786440 | tf_op jit(solution)/shard_map/ppermute | solution.py:10
  233.6 9.8 collective-permute-start
  245.8 9.8 collective-permute-start
  258.0 9.8 collective-permute-start
  270.2 9.8 collective-permute-start
  282.4 9.8 collective-permute-start
  294.6 9.8 collective-permute-start
  306.8 9.8 collective-permute-start
  318.9 9.8 collective-permute-start
  331.1 9.8 collective-permute-start
  343.3 9.8 collective-permute-start
  355.5 9.8 collective-permute-start
  367.7 9.8 collective-permute-start
  379.9 9.8 collective-permute-start
  392.1 9.8 collective-permute-start
  404.3 9.8 collective-permute-start
  416.5 9.8 collective-permute-start
  428.7 9.8 collective-permute-start
  440.9 9.8 collective-permute-start
  453.1 9.8 collective-permute-start
  465.3 9.8 collective-permute-start
  477.5 9.8 collective-permute-start
  489.7 9.8 collective-permute-start
  501.9 9.8 collective-permute-start
  514.0 9.8 collective-permute-start
  526.2 9.8 collective-permute-start
  538.4 9.8 collective-permute-start
  550.6 9.8 collective-permute-start
  562.8 9.8 collective-permute-start
  575.0 9.8 collective-permute-start
  587.2 9.8 collective-permute-start
  599.4 9.8 collective-permute-start
  611.6 9.8 collective-permute-start
  623.8 9.8 collective-permute-start
  636.0 9.8 collective-permute-start
  648.2 9.8 collective-permute-start
  660.4 9.8 collective-permute-start
  672.6 9.8 collective-permute-start
  684.8 9.8 collective-permute-start
  697.0 9.8 collective-permute-start
  709.1 9.8 collective-permute-start
  721.3 9.8 collective-permute-start
  733.5 9.8 collective-permute-start
  757.9 9.8 collective-permute-start
  818.9 9.8 collective-permute-start
  912.1 10.1 collective-permute-start.2
  915.4 219.2 %reduce-scatter.5.cloned.1.call-start = ((), (), s32[]{:S(2)}) async-start(), calls=%async_computation.3 | async-start | bytes 655360 | tf_op jit(solution)/shard_map/reduce_scatter | solution.py:94
  (92 other events, 343.4 us)
Sparse Core Ops, SparseCore 0:
  915.5 189.8 reduce-scatter.2
  1108.5 26.0 reduce-scatter.4
where the time goes:
time: 1150 us; the launch traced here: 1140 us
  waiting for transfers between devices  667 us (58%)
  matrix products  238 us (21%)
  starting transfers between devices  128 us (11%)
  other arithmetic  43.3 us (4%)
  local copies, waits for them, and re-layouts  41.8 us (4%)
  between operations  14.5 us (1%)
    ppermute x65, waiting for transfers between devices, passed_along(): return lax.ppermute(array, axis, pairs)  471 us
    dot_general x686, matrix products, matprod(): return jnp.matmul(left, right, precision=lax.Precision.HIGHEST)  238 us
    reduce_scatter x1, waiting for transfers between devices, on_device(): lax.psum_scatter(onsite, 'energy', scatter_dimension=1, tiled=True)  167 us
    ppermute x65, starting transfers between devices, passed_along(): return lax.ppermute(array, axis, pairs)  128 us
    reduce_scatter x1, waiting for transfers between devices, on_device(): lax.psum_scatter(coupling, 'energy', scatter_dimension=1, tiled=True)  29.2 us
  transfers between devices with their start and end apart: 67, of which 66 were waited for; matrix products, arithmetic and copies ran while one was open for 2% of the time, Pallas kernels for 0%

commit v1 on v0

v1 whole, which is shorter than its diff:
```python
import functools

import jax
import jax.numpy as jnp
from jax import lax
from jax.experimental import pallas as pl
from jax.experimental.pallas import tpu as pltpu
from jax.sharding import PartitionSpec as P

F32 = jnp.float32
BF16 = jnp.bfloat16
MESH = pl.DeviceIdType.MESH
B = 128
S = 8
ROWS = 32
NX, NY = 4, 4


def split(a):
    high = a.astype(BF16)
    return high, (a - high.astype(F32)).astype(BF16)


def dot(a, b, nt=False):
    return lax.dot_general(
        a, b, (((1,), (1 if nt else 0,)), ((), ())), preferred_element_type=F32
    )


def wide(b):
    re, im = b[:, :B], b[:, B:]
    return jnp.concatenate([b, jnp.concatenate([-im, re], 1)], 0)


def wide_t(b):
    re, im = b[:, :B], b[:, B:]
    return jnp.concatenate(
        [jnp.concatenate([re, -im], 1), jnp.concatenate([im, re], 1)], 0
    )


def lhs(x):
    high, low = split(x)
    return jnp.concatenate([high, low], 0)


def rhs(b):
    high, low = split(b)
    return wide(high), wide(low)


def rhs_t(b):
    high, low = split(b)
    return wide_t(high), wide_t(low)


def mul(x, w, nt=False):
    rows = x.shape[0] // 2
    y = dot(x, w[0], nt)
    return y[:rows] + y[rows:] + dot(x[:rows], w[1], nt)


def apply_map(off, prod, inner):
    return off + mul(lhs(mul(lhs(prod), rhs(inner))), rhs_t(prod), True)


def combine(first, second):
    off1, p1 = first
    off2, p2 = second
    left = lhs(p1)
    y = mul(left, rhs(off2))
    prod = mul(left, rhs(p2))
    return off1 + mul(lhs(y), rhs_t(p1), True), prod


def kernel(
    g_hbm, u_hbm, c_hbm, on_ref, cp_ref,
    g, u, c, link, own, tbuf, xs, ys, ex, ey, zbuf, dbuf, zrecv, xin,
    ap, gt, w0, q, gg, vv, xt, w, part, recv,
    in_sem, halo_sem, pair_sem, x_send, x_recv, y_send, y_recv, z_sem, d_sem, r_send, r_recv,
):
    s = lax.axis_index("slab")
    e = lax.axis_index("energy")
    core = lax.rem(s, 2)
    x = lax.rem(s // 2, NX)
    y = lax.rem(s // (2 * NX), NY)
    z = s // (2 * NX * NY)
    slabs = 2 * NX * NY * 2
    prev = lax.rem(s + slabs - 1, slabs)
    after = lax.rem(s + 1, slabs)
    partner = s + 1 - 2 * core
    zpeer = lax.rem(s + slabs // 2, slabs)

    def xpeer(d):
        return s + (lax.rem(x + d, NX) - x) * 2

    def ypeer(d):
        return s + (lax.rem(y + d, NY) - y) * (2 * NX)

    def epeer(d):
        return lax.rem(e + d, 4)

    cg = pltpu.make_async_copy(g_hbm, g.at[pl.ds(0, S)], in_sem.at[0])
    cu = pltpu.make_async_copy(u_hbm, u, in_sem.at[1])
    cc = pltpu.make_async_copy(c_hbm, c, in_sem.at[2])
    cg.start()
    cu.start()
    cc.start()

    barrier = pltpu.get_barrier_semaphore()
    greet = [(prev, e), (after, e), (partner, e), (zpeer, e)]
    greet += [(xpeer(d), e) for d in (1, 2, 3)]
    greet += [(ypeer(d), e) for d in (1, 2, 3)]
    greet += [(s, epeer(d)) for d in (1, 2, 3)]
    for device in greet:
        pl.semaphore_signal(barrier, inc=1, device_id=device, device_id_type=MESH)
    pl.semaphore_wait(barrier, len(greet))

    def remote(src, dst, send, recv_, device):
        return pltpu.make_async_remote_copy(
            src_ref=src, dst_ref=dst, send_sem=send, recv_sem=recv_,
            device_id=device, device_id_type=MESH,
        )

    halo = remote(g_hbm.at[0], g.at[S], halo_sem.at[0], halo_sem.at[1], (prev, e))
    halo.start()

    def cat(ref, i, k):
        return jnp.concatenate([ref[i, k, 0], ref[i, k, 1]], 1)

    def make_links(i, scale=None):
        ui = u[i]
        if scale is not None:
            ui = ui * scale
        uu = lhs(ui)
        out = []
        for k in range(2):
            gh, gl = split(jnp.concatenate([g[i + 1, k, 0], g[i + 1, k, 1]], 0))
            value = mul(uu, (gh, gl), True)
            link[i, k] = value
            out.append(value)
        return out

    cg.wait()
    cu.wait()
    first = make_links(0)
    cc.wait()
    for k in range(2):
        own[k, 0] = cat(c, 0, k)
        own[k, 1] = first[k]

    def fold(i, carry):
        links = make_links(i)
        for k in range(2):
            pk = own[k, 1]
            left = lhs(pk)
            yk = mul(left, rhs(cat(c, i, k)))
            own[k, 1] = mul(left, rhs(links[k]))
            own[k, 0] += mul(lhs(yk), rhs_t(pk), True)
        return carry

    lax.fori_loop(1, S - 1, fold, 0)
    halo.wait_recv()
    links = make_links(S - 1, jnp.where(s == slabs - 1, 0.0, 1.0).astype(F32))
    for k in range(2):
        pk = own[k, 1]
        left = lhs(pk)
        yk = mul(left, rhs(cat(c, S - 1, k)))
        own[k, 1] = mul(left, rhs(links[k]))
        own[k, 0] += mul(lhs(yk), rhs_t(pk), True)

    pair = remote(
        own.at[1 - core], tbuf.at[core], pair_sem.at[0], pair_sem.at[1], (partner, e)
    )
    pair.start()
    tbuf[core] = own[core]
    pair.wait_recv()

    def both(ref, i):
        return ref[i, 0], ref[i, 1]

    def put(ref, i, value):
        ref[i, 0] = value[0]
        ref[i, 1] = value[1]

    put(xs, x, combine(both(tbuf, 0), both(tbuf, 1)))

    def gather(ref, me, peer, send, recv_):
        out = []
        for d in (1, 2, 3):
            copy = remote(
                ref.at[me], ref.at[me], send.at[d - 1], recv_.at[d - 1], (peer(d), e)
            )
            copy.start()
            out.append(copy)
        return out

    x_copies = gather(xs, x, xpeer, x_send, x_recv)

    def flip(i):
        for k in range(2):
            gt[i, k] = jnp.concatenate([g[i, k, 0].T, g[i, k, 1].T], 1)

    def prepare(i):
        flip(i)
        uh, ul = split(u[i])
        uu = jnp.concatenate([uh, ul], 1)
        for k in range(2):
            a0, ps = ap[k, 0], ap[k, 1]
            gi, gti = cat(g, i, k), gt[i, k]
            lg = lhs(gi)
            lt = lhs(gti)
            h0 = mul(lt, rhs(a0))
            w0[i, k] = mul(lhs(h0), rhs(gti))
            pw = rhs(ps)
            q[i, k] = lhs(mul(lt, pw))
            gg[i, k] = mul(lg, pw)
            rows = [gi[:, :B], -gi[:, B:], gti[:, :B], -gti[:, B:]]
            xh, xl = split(jnp.concatenate(rows, 0))
            t = dot(xh, uu)
            vh, vl = split(t[:, :B] + t[:, B:] + dot(xl, uh))
            for n in range(4):
                column = (n // 2) * 512 + k * 256 + (n % 2) * B
                vv[i, 0:B, column : column + B] = vh[n * B : n * B + B]
                vv[i, B : 2 * B, column : column + B] = vl[n * B : n * B + B]

    def step_back(i):
        for k in range(2):
            lk = link[i, k]
            left = lhs(lk)
            yk = mul(left, rhs(ap[k, 0]))
            pk = mul(left, rhs(ap[k, 1]))
            ap[k, 1] = pk
            ap[k, 0] = cat(c, i, k) + mul(lhs(yk), rhs_t(lk), True)

    for k in range(2):
        ap[k, 0] = cat(c, S - 1, k)
        ap[k, 1] = link[S - 1, k]
    flip(S)
    for k in range(2):
        w0[S, k] = jnp.zeros((B, 2 * B), F32)
        q[S, k] = lhs(gt[S, k])
        gg[S, k] = cat(g, S, k)
    prepare(S - 1)

    def shadow(j, carry):
        i = S - 2 - j
        step_back(i)
        prepare(i)
        return carry

    lax.fori_loop(0, 3, shadow, 0)

    def finish(copies):
        for copy in copies:
            copy.wait_recv()

    def level_total(ref):
        t01 = combine(both(ref, 0), both(ref, 1))
        t23 = combine(both(ref, 2), both(ref, 3))
        return t23, combine(t01, t23)

    row_i = lax.broadcasted_iota(jnp.int32, (B, 2 * B), 0)
    col_i = lax.broadcasted_iota(jnp.int32, (B, 2 * B), 1)
    unit = jnp.where(row_i == col_i, 1.0, 0.0).astype(F32)

    def later(ref, out, t23):
        put(out, 0, combine(both(ref, 1), t23))
        put(out, 1, t23)
        out[2] = ref[3]
        out[3, 0] = jnp.zeros((B, 2 * B), F32)
        out[3, 1] = unit

    finish(x_copies)
    t23, total = level_total(xs)
    put(ys, y, total)
    y_copies = gather(ys, y, ypeer, y_send, y_recv)
    later(xs, ex, t23)
    lax.fori_loop(3, S - 1, shadow, 0)

    finish(y_copies)
    t23, total = level_total(ys)
    zbuf[...] = total[0]
    zcopy = remote(zbuf, zrecv, z_sem.at[0], z_sem.at[1], (zpeer, e))

    @pl.when(z == 1)
    def _():
        zcopy.start()
        zrecv[...] = jnp.zeros((B, 2 * B), F32)

    later(ys, ey, t23)
    outer = combine(both(ex, x), both(ey, y))
    inner = combine(both(tbuf, 1), outer)

    @pl.when(z == 0)
    def _():
        zcopy.wait_recv()

    top = zrecv[...]
    chip_in = apply_map(outer[0], outer[1], top)
    core_in = apply_map(inner[0], inner[1], top)
    is_first = core == 0
    dbuf[...] = jnp.where(is_first, chip_in, core_in)
    down = remote(dbuf, xin.at[core], d_sem.at[0], d_sem.at[1], (partner, e))
    down.start()
    xin[core] = jnp.where(is_first, core_in, chip_in)
    down.wait_recv()

    for k in range(2):
        high, low = rhs(xin[k])
        xt[k, 0] = high
        xt[k, 1] = low

    def weights(i):
        for k in range(2):
            zk = mul(q[i, k], (xt[k, 0], xt[k, 1]))
            w[i, k] = w0[i, k] + mul(lhs(zk), rhs_t(gg[i, k]), True)

    weights(S)

    def finals(j, carry):
        i = S - 1 - j
        wh0, wl0 = split(w[i + 1, 0])
        wh1, wl1 = split(w[i + 1, 1])
        nt = jnp.concatenate(
            [jnp.concatenate([wh0, wh1], 1), jnp.concatenate([wl0, wl1], 1)], 0
        )
        nn = jnp.concatenate(
            [
                jnp.concatenate([h[:, m : m + B], l[:, m : m + B]], 1)
                for h, l in ((wh0, wl0), (wh1, wl1))
                for m in (0, B)
            ],
            0,
        )
        t = dot(vv[i, :, 0:512], nt, True) + dot(vv[i, :, 512:1024], nn)
        coupling = t[:B, :B] + (t[:B, B:] + t[B:, :B])
        weights(i)
        onsite = w[i, 0, :, 0:B] + w[i, 1, :, 0:B]
        for r in range(4):
            part[i, r, 0] = onsite[r * ROWS : (r + 1) * ROWS]
            part[i, r, 1] = coupling[r * ROWS : (r + 1) * ROWS]
        for d in (1, 2, 3):
            spread(i, d).start()
        return carry

    def spread(i, d):
        return remote(
            part.at[i, epeer(d)], recv.at[i, d - 1],
            r_send.at[i, d - 1], r_recv.at[i, d - 1], (s, epeer(d)),
        )

    lax.fori_loop(0, S, finals, 0)

    def collect(j, carry):
        i = S - 1 - j
        for d in (1, 2, 3):
            spread(i, d).wait_recv()
        total_i = part[i, e] + recv[i, 0] + (recv[i, 1] + recv[i, 2])
        on_ref[i] = total_i[0]
        cp_ref[i] = total_i[1]
        return carry

    lax.fori_loop(0, S, collect, 0)

    halo.wait_send()
    pair.wait_send()
    for copy in x_copies + y_copies:
        copy.wait_send()

    @pl.when(z == 1)
    def _():
        zcopy.wait_send()

    down.wait_send()

    def drain(i, carry):
        for d in (1, 2, 3):
            spread(i, d).wait_send()
        return carry

    lax.fori_loop(0, S, drain, 0)


def on_device(green_blocks, couplings, green_cotangent):
    shape = (S, 2, 2, B, B)
    block = (B, 2 * B)
    vmem = pltpu.VMEM
    out = jax.ShapeDtypeStruct((S, ROWS, B), F32)
    dma = pltpu.SemaphoreType.DMA
    return pl.pallas_call(
        kernel,
        out_shape=(out, out),
        in_specs=[pl.BlockSpec(memory_space=pl.ANY)] * 3,
        out_specs=(pl.BlockSpec(memory_space=vmem),) * 2,
        scratch_shapes=[
            vmem((S + 1, 2, 2, B, B), F32),
            vmem((S, B, B), F32),
            vmem(shape, F32),
            vmem((S, 2) + block, F32),
            vmem((2, 2) + block, F32),
            vmem((2, 2) + block, F32),
            vmem((NX, 2) + block, F32),
            vmem((NY, 2) + block, F32),
            vmem((NX, 2) + block, F32),
            vmem((NY, 2) + block, F32),
            vmem(block, F32),
            vmem(block, F32),
            vmem(block, F32),
            vmem((2,) + block, F32),
            vmem((2, 2) + block, F32),
            vmem((S + 1, 2) + block, F32),
            vmem((S + 1, 2) + block, F32),
            vmem((S + 1, 2, 2 * B, 2 * B), BF16),
            vmem((S + 1, 2) + block, F32),
            vmem((S, 2 * B, 8 * B), BF16),
            vmem((2, 2, 2 * B, 2 * B), BF16),
            vmem((S + 1, 2) + block, F32),
            vmem((S, 4, 2, ROWS, B), F32),
            vmem((S, 3, 2, ROWS, B), F32),
            dma((3,)),
            dma((2,)),
            dma((2,)),
            dma((3,)),
            dma((3,)),
            dma((3,)),
            dma((3,)),
            dma((2,)),
            dma((2,)),
            dma((S, 3)),
            dma((S, 3)),
        ],
        compiler_params=pltpu.CompilerParams(
            collective_id=0, has_side_effects=True, vmem_limit_bytes=50 * 1024 * 1024
        ),
    )(
        green_blocks.reshape(shape),
        couplings,
        green_cotangent.reshape(shape),
    )


def solution(mesh):
    in_specs = (
        P("slab", "energy", None, None, None, None),
        P("slab", None, None),
        P("slab", "energy", None, None, None, None),
    )
    out_specs = (P("slab", "energy", None), P("slab", "energy", None))
    return jax.shard_map(
        on_device, mesh=mesh, in_specs=in_specs, out_specs=out_specs, check_vma=False
    )
```

time: 1150 us -> 84.1 us (0.07)
  waiting for transfers between devices: 667 us -> 0 us
  matrix products: 238 us -> 0 us
  starting transfers between devices: 128 us -> 0 us
  Pallas kernels: 0 us -> 79.3 us
  other arithmetic: 43.3 us -> 0 us
  local copies, waits for them, and re-layouts: 41.8 us -> 3.94 us
  between operations: 14.5 us -> 0.65 us
    ppermute x65 -> x0, waiting for transfers between devices: 471 us -> none  [passed_along(): return lax.ppermute(array, axis, pairs)]
    dot_general x686 -> x0, matrix products: 238 us -> none  [matprod(): return jnp.matmul(left, right, precision=lax.Precision.HIGHEST)]
    reduce_scatter x2 -> x0, waiting for transfers between devices: 196 us -> none  [the longest x1 167 us: on_device(): lax.psum_scatter(onsite, 'energy', scatter_dimension=1, tiled=True)]
    ppermute x65 -> x0, starting transfers between devices: 128 us -> none  [passed_along(): return lax.ppermute(array, axis, pairs)]
    pallas_call x0 -> x1, Pallas kernels: none -> 79.3 us  [on_device(): pl.pallas_call(kernel, out_shape=(out, out), in_specs=[pl.BlockSpec(memor...]
    add x87 -> x0, other arithmetic: 32 us -> none  [the longest x16 15.7 us: expand_slab(): adjoint_now = cotangent + sandwich(link_now, adjoint_next)]
    transpose x16 -> x0, local copies, waits for them, and re-layouts: 15.8 us -> none  [flipped(): return jnp.swapaxes(value, -1, -2)]
  transfers between devices with their start and end apart: 67 -> 0, of which waited for: 66 -> 0; matrix products, arithmetic and copies ran while one was open for 2% -> 0% of each run, Pallas kernels for 0% -> 0%
where the time goes in v1:
time: 84.1 us; the launch traced here: 83.9 us
  Pallas kernels  79.3 us (94%)
  local copies, waits for them, and re-layouts  3.94 us (5%)
    pallas_call x1, Pallas kernels, on_device(): pl.pallas_call(kernel, out_shape=(out, out), in_specs=[pl.BlockSpec(memor...  79.3 us
    unnamed x6, local copies, waits for them, and re-layouts  3.94 us

profile of v1, /device:TPU:1, one launch (start us, length us, event | category | flops | bytes accessed | tf_op | source)
XLA Modules:
  0.0 83.9 jit_solution(16982051800498214415)
XLA Ops:
  0.6 0.0 copy-start
  0.6 1.6 %copy-done = f32[8,1,2,2,128,128]{5,4,3,2,1,0:T(8,128)S(1)} copy-done((f32[8,1,2,2,128,128]{5,4,3,2,1,0:T(8,128)S(1)}, f32[8,1,2,2,128,128]{5,4,3,2,1,0:T(8,128)}, u32[]{:S(2)}) %copy-start) | copy-done | bytes 2097176
  2.2 0.0 copy-start.1
  2.2 1.0 %copy-done.1 = f32[8,128,128]{2,1,0:T(8,128)S(1)} copy-done((f32[8,128,128]{2,1,0:T(8,128)S(1)}, f32[8,128,128]{2,1,0:T(8,128)}, u32[]{:S(2)}) %copy-start.1) | copy-done | bytes 524312
  3.3 79.3 %shard_map.50 = (f32[8,32,128]{2,1,0:T(8,128)S(1)}, f32[8,32,128]{2,1,0:T(8,128)S(1)}) custom-call(f32[8,2,2,128,128]{4,3,2,1,0:T(8,128)S(1)} %bitcast.2, f32[8,128,128]{2,1,0:T(8,128)S(1)} %copy-done.1, f32[8,2,2,128,128]{4,3,2,1,0:T(8,128)} %bitcast.3), custom_call_target="tpu_custom_call" | custom-call | tf_op jit(solution)/shard_map/pallas_call | solution.py:391
  82.6 0.7 copy.7
  83.2 0.7 copy.8
Async XLA Ops:
  0.6 1.6 %copy-start = (f32[8,1,2,2,128,128]{5,4,3,2,1,0:T(8,128)S(1)}, f32[8,1,2,2,128,128]{5,4,3,2,1,0:T(8,128)}, u32[]{:S(2)}) copy-start(f32[8,1,2,2,128,128]{5,4,3,2,1,0:T(8,128)} %param.3) | copy-start | bytes 6291460
  2.2 1.0 %copy-start.1 = (f32[8,128,128]{2,1,0:T(8,128)S(1)}, f32[8,128,128]{2,1,0:T(8,128)}, u32[]{:S(2)}) copy-start(f32[8,128,128]{2,1,0:T(8,128)} %u_hbm.1) | copy-start | bytes 1572868

commit v2 on v1

v2 whole, which is shorter than its diff:
```python
import functools

import jax
import jax.numpy as jnp
from jax import lax
from jax.experimental import pallas as pl
from jax.experimental.pallas import tpu as pltpu
from jax.sharding import PartitionSpec as P

F32 = jnp.float32
BF16 = jnp.bfloat16
MESH = pl.DeviceIdType.MESH
B = 128
S = 8
ROWS = 32
NX, NY = 4, 4


def split(a):
    high = a.astype(BF16)
    return high, (a - high.astype(F32)).astype(BF16)


def dot(a, b, nt=False):
    return lax.dot_general(
        a, b, (((1,), (1 if nt else 0,)), ((), ())), preferred_element_type=F32
    )


def wide(b):
    re, im = b[:, :B], b[:, B:]
    return jnp.concatenate([b, jnp.concatenate([-im, re], 1)], 0)


def wide_t(b):
    re, im = b[:, :B], b[:, B:]
    return jnp.concatenate(
        [jnp.concatenate([re, -im], 1), jnp.concatenate([im, re], 1)], 0
    )


def lhs(x):
    high, low = split(x)
    return jnp.concatenate([high, low], 0)


def rhs(b):
    high, low = split(b)
    return wide(high), wide(low)


def rhs_t(b):
    high, low = split(b)
    return wide_t(high), wide_t(low)


def mul(x, w, nt=False):
    rows = x.shape[0] // 2
    y = dot(x, w[0], nt)
    return y[:rows] + y[rows:] + dot(x[:rows], w[1], nt)


def apply_map(off, prod, inner):
    return off + mul(lhs(mul(lhs(prod), rhs(inner))), rhs_t(prod), True)


def combine(first, second):
    off1, p1 = first
    off2, p2 = second
    left = lhs(p1)
    y = mul(left, rhs(off2))
    prod = mul(left, rhs(p2))
    return off1 + mul(lhs(y), rhs_t(p1), True), prod


def kernel(
    g_hbm, u_hbm, c_hbm, on_ref, cp_ref,
    g, u, c, link, pre, own, tbuf, xs, ys, ex, ey, lp, lo, zbuf, dbuf, zrecv, xin,
    ap, gt, w0, q, gg, vv, xt, w, part, relay, recv,
    g_sem, in_sem, pair_sem, x_send, x_recv, y_send, y_recv, z_sem, d_sem, h_sem,
    r_send, r_recv,
):
    s = lax.axis_index("slab")
    e = lax.axis_index("energy")
    core = lax.rem(s, 2)
    x = lax.rem(s // 2, NX)
    y = lax.rem(s // (2 * NX), NY)
    z = s // (2 * NX * NY)
    slabs = 2 * NX * NY * 2
    prev = lax.rem(s + slabs - 1, slabs)
    after = lax.rem(s + 1, slabs)
    partner = s + 1 - 2 * core
    zpeer = lax.rem(s + slabs // 2, slabs)
    last = s == slabs - 1

    def xpeer(d):
        return s + (lax.rem(x + d, NX) - x) * 2

    def ypeer(d):
        return s + (lax.rem(y + d, NY) - y) * (2 * NX)

    def epeer(d):
        return lax.rem(e + d, 4)

    barrier = pltpu.get_barrier_semaphore()
    greet = [(prev, e), (after, e), (partner, e), (zpeer, e)]
    greet += [(xpeer(d), e) for d in (1, 3)]
    greet += [(ypeer(d), e) for d in (1, 3)]
    greet += [(s, epeer(d)) for d in (1, 3)]
    for device in greet:
        pl.semaphore_signal(barrier, inc=1, device_id=device, device_id_type=MESH)

    def g_copy(i):
        return pltpu.make_async_copy(g_hbm.at[i], g.at[i], g_sem.at[i])

    cu = pltpu.make_async_copy(u_hbm, u, in_sem.at[0])
    cc = pltpu.make_async_copy(c_hbm, c, in_sem.at[1])
    g_copy(0).start()
    cu.start()
    for i in range(1, S):
        g_copy(i).start()
    cc.start()

    def remote(src, dst, send, recv_, device):
        return pltpu.make_async_remote_copy(
            src_ref=src, dst_ref=dst, send_sem=send, recv_sem=recv_,
            device_id=device, device_id_type=MESH,
        )

    def cat(ref, i, k):
        return jnp.concatenate([ref[i, k, 0], ref[i, k, 1]], 1)

    def flip(i):
        for k in range(2):
            gt[i, k] = jnp.concatenate([g[i, k, 0].T, g[i, k, 1].T], 1)

    g_copy(0).wait()
    flip(0)
    for k in range(2):
        pre[0, k] = gt[0, k]
    cu.wait()

    def chain(i, carry):
        g_copy(i + 1).wait()
        uu = lhs(u[i])
        for k in range(2):
            gh, gl = split(jnp.concatenate([g[i + 1, k, 0], g[i + 1, k, 1]], 0))
            value = mul(uu, (gh, gl), True)
            link[i, k] = value
            pre[i + 1, k] = mul(lhs(pre[i, k]), rhs(value))
        return carry

    lax.fori_loop(0, S - 1, chain, 0)
    last_u = u[S - 1] * jnp.where(last, 0.0, 1.0).astype(F32)
    uw = split(last_u)
    for k in range(2):
        value = pre[S - 1, k]
        t = mul(lhs(jnp.concatenate([value[:, :B], value[:, B:]], 0)), uw)
        own[k, 1] = jnp.concatenate([t[:B], t[B:]], 1)

    pl.semaphore_wait(barrier, len(greet))

    def pair(t):
        return remote(
            own.at[1 - core, t], tbuf.at[core, t],
            pair_sem.at[0, t], pair_sem.at[1, t], (partner, e),
        )

    pair(1).start()
    tbuf[core, 1] = own[core, 1]
    cc.wait()
    for k in range(2):
        own[k, 0] = jnp.zeros((B, 2 * B), F32)

    def fold(i, carry):
        for k in range(2):
            pk = pre[i, k]
            yk = mul(lhs(pk), rhs(cat(c, i, k)))
            own[k, 0] += mul(lhs(yk), rhs_t(pk), True)
        return carry

    class Ring:
        def __init__(self, ref, t, me, peer, send, recv_):
            self.ref, self.t, self.me, self.peer = ref, t, me, peer
            self.send, self.recv = send, recv_

        def copy(self, n, arriving=False):
            step = (1, 1, 3, 3, 1, 3)[n]
            half = (0, 1, 1, 0, 0, 1)[n]
            slot = self.me if n < 4 else lax.rem(self.me + 4 - step, 4)
            target = slot
            if arriving:
                target = lax.rem(self.me + 4 - step, 4) if n < 4 else lax.rem(self.me + 2, 4)
            at = pl.ds(half * (B // 2), B // 2)
            return remote(
                self.ref.at[slot, self.t, at], self.ref.at[target, self.t, at],
                self.send.at[self.t, n], self.recv.at[self.t, n], (self.peer(step), e),
            )

        def start(self):
            for n in (0, 2, 1, 3):
                self.copy(n).start()

        def forward(self):
            self.copy(0, True).wait_recv()
            self.copy(4).start()
            self.copy(2, True).wait_recv()
            self.copy(5).start()

        def finish(self):
            for n in (1, 3, 4, 5):
                self.copy(n, True).wait_recv()

        def drain(self):
            for n in range(6):
                self.copy(n).wait_send()

    xo = Ring(xs, 0, x, xpeer, x_send, x_recv)
    xp = Ring(xs, 1, x, xpeer, x_send, x_recv)
    yo = Ring(ys, 0, y, ypeer, y_send, y_recv)
    yp = Ring(ys, 1, y, ypeer, y_send, y_recv)

    def prod(p1, p2):
        return mul(lhs(p1), rhs(p2))

    FOLD_CUT = 4
    lax.fori_loop(0, FOLD_CUT, fold, 0)
    pair(1).wait_recv()
    xs[x, 1] = prod(tbuf[0, 1], tbuf[1, 1])
    xp.start()
    lax.fori_loop(FOLD_CUT, S, fold, 0)
    pair(0).start()
    tbuf[core, 0] = own[core, 0]
    xp.forward()
    pair(0).wait_recv()
    xs[x, 0] = apply_map(tbuf[0, 0], tbuf[0, 1], tbuf[1, 0])
    xo.start()

    def prepare(i):
        flip(i)
        uh, ul = split(u[i])
        uu = jnp.concatenate([uh, ul], 1)
        for k in range(2):
            a0, ps = ap[k, 0], ap[k, 1]
            gi, gti = cat(g, i, k), gt[i, k]
            lg = lhs(gi)
            lt = lhs(gti)
            h0 = mul(lt, rhs(a0))
            w0[i, k] = mul(lhs(h0), rhs(gti))
            pw = rhs(ps)
            q[i, k] = lhs(mul(lt, pw))
            gg[i, k] = mul(lg, pw)
            rows = [gi[:, :B], -gi[:, B:], gti[:, :B], -gti[:, B:]]
            xh, xl = split(jnp.concatenate(rows, 0))
            t = dot(xh, uu)
            vh, vl = split(t[:, :B] + t[:, B:] + dot(xl, uh))
            for n in range(4):
                column = (n // 2) * 512 + k * 256 + (n % 2) * B
                vv[i, 0:B, column : column + B] = vh[n * B : n * B + B]
                vv[i, B : 2 * B, column : column + B] = vl[n * B : n * B + B]

    def step_back(i):
        for k in range(2):
            lk = link[i, k]
            left = lhs(lk)
            yk = mul(left, rhs(ap[k, 0]))
            pk = mul(left, rhs(ap[k, 1]))
            ap[k, 1] = pk
            ap[k, 0] = cat(c, i, k) + mul(lhs(yk), rhs_t(lk), True)

    zero = jnp.zeros((B, 2 * B), F32)
    for k in range(2):
        ap[k, 0] = cat(c, S - 1, k)
        ap[k, 1] = jnp.concatenate([last_u, jnp.zeros((B, B), F32)], 1)

    def level_p(ref, n):
        lp[n, 0] = prod(ref[0, 1], ref[1, 1])
        lp[n, 1] = prod(ref[2, 1], ref[3, 1])

    def level_o(ref, n):
        o01 = apply_map(ref[0, 0], ref[0, 1], ref[1, 0])
        o23 = apply_map(ref[2, 0], ref[2, 1], ref[3, 0])
        lo[n] = o23
        return apply_map(o01, lp[n, 0], o23)

    row_i = lax.broadcasted_iota(jnp.int32, (B, 2 * B), 0)
    col_i = lax.broadcasted_iota(jnp.int32, (B, 2 * B), 1)
    unit = jnp.where(row_i == col_i, 1.0, 0.0).astype(F32)

    def later(ref, out, n):
        o, p = combine((ref[1, 0], ref[1, 1]), (lo[n], lp[n, 1]))
        out[0, 0] = o
        out[0, 1] = p
        out[1, 0] = lo[n]
        out[1, 1] = lp[n, 1]
        out[2] = ref[3]
        out[3, 0] = zero
        out[3, 1] = unit

    zcopy = remote(zbuf, zrecv, z_sem.at[0], z_sem.at[1], (zpeer, e))

    def shadow(j, carry):
        i = S - 1 - j

        @pl.when(j > 0)
        def _():
            step_back(i)

        prepare(i)

        @pl.when(j == 0)
        def _():
            xp.finish()
            level_p(xs, 0)
            ys[y, 1] = prod(lp[0, 0], lp[0, 1])
            yp.start()

        @pl.when(j == 1)
        def _():
            xo.forward()

        @pl.when(j == 2)
        def _():
            yp.forward()

        @pl.when(j == 3)
        def _():
            xo.finish()
            ys[y, 0] = level_o(xs, 0)
            yo.start()
            yp.finish()
            level_p(ys, 1)

        @pl.when(j == 4)
        def _():
            yo.forward()
            later(xs, ex, 0)

        @pl.when(j == 6)
        def _():
            yo.finish()
            zbuf[...] = level_o(ys, 1)

            @pl.when(z == 1)
            def _():
                zcopy.start()
                zrecv[...] = zero

        return carry

    lax.fori_loop(0, S, shadow, 0)

    later(ys, ey, 1)
    outer = combine((ex[x, 0], ex[x, 1]), (ey[y, 0], ey[y, 1]))
    inner = combine((tbuf[1, 0], tbuf[1, 1]), outer)

    @pl.when(z == 0)
    def _():
        zcopy.wait_recv()

    top = zrecv[...]
    chip_in = apply_map(outer[0], outer[1], top)
    core_in = apply_map(inner[0], inner[1], top)
    is_first = core == 0
    dbuf[...] = jnp.where(is_first, chip_in, core_in)
    down = remote(dbuf, xin.at[core], d_sem.at[0], d_sem.at[1], (partner, e))
    down.start()
    xin[core] = jnp.where(is_first, core_in, chip_in)
    down.wait_recv()

    for k in range(2):
        high, low = rhs(xin[k])
        xt[k, 0] = high
        xt[k, 1] = low

    def weights(i):
        for k in range(2):
            zk = mul(q[i, k], (xt[k, 0], xt[k, 1]))
            w[i, k] = w0[i, k] + mul(lhs(zk), rhs_t(gg[i, k]), True)

    weights(0)
    halo = remote(w.at[0], w.at[S], h_sem.at[0], h_sem.at[1], (prev, e))
    halo.start()

    def spread(i, n):
        step = (3, 1, 1, 3)[n]
        kind = (0, 1, 0, 1)[n]
        owner = epeer(2) if n < 2 else epeer(step)
        target = relay.at[i, kind] if n < 2 else recv.at[i, 0, kind]
        return remote(
            part.at[i, owner, kind], target,
            r_send.at[i, n], r_recv.at[i, n], (s, epeer(step)),
        )

    def pass_on(i, kind):
        step = (3, 1)[kind]
        return remote(
            relay.at[i, kind], recv.at[i, 1, kind],
            r_send.at[i, 4 + kind], r_recv.at[i, 4 + kind], (s, epeer(step)),
        )

    def finals(i, carry):
        @pl.when(i < S - 1)
        def _():
            weights(i + 1)

        @pl.when(i == S - 1)
        def _():
            halo.wait_recv()

            @pl.when(last)
            def _():
                for k in range(2):
                    w[S, k] = zero

        wh0, wl0 = split(w[i + 1, 0])
        wh1, wl1 = split(w[i + 1, 1])
        nt = jnp.concatenate(
            [jnp.concatenate([wh0, wh1], 1), jnp.concatenate([wl0, wl1], 1)], 0
        )
        nn = jnp.concatenate(
            [
                jnp.concatenate([h[:, m : m + B], l[:, m : m + B]], 1)
                for h, l in ((wh0, wl0), (wh1, wl1))
                for m in (0, B)
            ],
            0,
        )
        t = dot(vv[i, :, 0:512], nt, True) + dot(vv[i, :, 512:1024], nn)
        coupling = t[:B, :B] + (t[:B, B:] + t[B:, :B])
        onsite = w[i, 0, :, 0:B] + w[i, 1, :, 0:B]
        for r in range(4):
            part[i, r, 0] = onsite[r * ROWS : (r + 1) * ROWS]
            part[i, r, 1] = coupling[r * ROWS : (r + 1) * ROWS]
        for n in range(4):
            spread(i, n).start()
        return carry

    lax.fori_loop(0, S, finals, 0)

    def pass_all(i, carry):
        for kind, step in ((0, 3), (1, 1)):
            spread(i, kind).wait_recv()
            relay[i, kind] += part[i, epeer(step), kind]
            pass_on(i, kind).start()
        return carry

    lax.fori_loop(0, S, pass_all, 0)

    def collect(i, carry):
        for kind, out in ((0, on_ref), (1, cp_ref)):
            spread(i, 2 + kind).wait_recv()
            pass_on(i, kind).wait_recv()
            out[i] = part[i, e, kind] + recv[i, 0, kind] + recv[i, 1, kind]
        return carry

    lax.fori_loop(0, S, collect, 0)

    for t in range(2):
        pair(t).wait_send()
    for ring in (xp, xo, yp, yo):
        ring.drain()

    @pl.when(z == 1)
    def _():
        zcopy.wait_send()

    down.wait_send()
    halo.wait_send()

    def drain(i, carry):
        for n in range(4):
            spread(i, n).wait_send()
        for kind in range(2):
            pass_on(i, kind).wait_send()
        return carry

    lax.fori_loop(0, S, drain, 0)


def on_device(green_blocks, couplings, green_cotangent):
    shape = (S, 2, 2, B, B)
    block = (B, 2 * B)
    vmem = pltpu.VMEM
    out = jax.ShapeDtypeStruct((S, ROWS, B), F32)
    dma = pltpu.SemaphoreType.DMA
    return pl.pallas_call(
        kernel,
        out_shape=(out, out),
        in_specs=[pl.BlockSpec(memory_space=pl.ANY)] * 3,
        out_specs=(pl.BlockSpec(memory_space=vmem),) * 2,
        scratch_shapes=[
            vmem(shape, F32),
            vmem((S, B, B), F32),
            vmem(shape, F32),
            vmem((S, 2) + block, F32),
            vmem((S, 2) + block, F32),
            vmem((2, 2) + block, F32),
            vmem((2, 2) + block, F32),
            vmem((NX, 2) + block, F32),
            vmem((NY, 2) + block, F32),
            vmem((NX, 2) + block, F32),
            vmem((NY, 2) + block, F32),
            vmem((2, 2) + block, F32),
            vmem((2,) + block, F32),
            vmem(block, F32),
            vmem(block, F32),
            vmem(block, F32),
            vmem((2,) + block, F32),
            vmem((2, 2) + block, F32),
            vmem((S, 2) + block, F32),
            vmem((S, 2) + block, F32),
            vmem((S, 2, 2 * B, 2 * B), BF16),
            vmem((S, 2) + block, F32),
            vmem((S, 2 * B, 8 * B), BF16),
            vmem((2, 2, 2 * B, 2 * B), BF16),
            vmem((S + 1, 2) + block, F32),
            vmem((S, 4, 2, ROWS, B), F32),
            vmem((S, 2, ROWS, B), F32),
            vmem((S, 2, 2, ROWS, B), F32),
            dma((S,)),
            dma((2,)),
            dma((2, 2)),
            dma((2, 6)),
            dma((2, 6)),
            dma((2, 6)),
            dma((2, 6)),
            dma((2,)),
            dma((2,)),
            dma((2,)),
            dma((S, 6)),
            dma((S, 6)),
        ],
        compiler_params=pltpu.CompilerParams(
            collective_id=0, has_side_effects=True, vmem_limit_bytes=62 * 1024 * 1024
        ),
    )(
        green_blocks.reshape(shape),
        couplings,
        green_cotangent.reshape(shape),
    )


def solution(mesh):
    in_specs = (
        P("slab", "energy", None, None, None, None),
        P("slab", None, None),
        P("slab", "energy", None, None, None, None),
    )
    out_specs = (P("slab", "energy", None), P("slab", "energy", None))
    return jax.shard_map(
        on_device, mesh=mesh, in_specs=in_specs, out_specs=out_specs, check_vma=False
    )
```

time: 84.1 us -> 72.8 us (0.87)
  Pallas kernels: 79.3 us -> 68.1 us
    pallas_call x1, Pallas kernels: 79.3 us -> 68.1 us  [on_device(): pl.pallas_call(kernel, out_shape=(out, out), in_specs=[pl.BlockSpec(memor...]
    unnamed x6 -> x2, local copies, waits for them, and re-layouts: 3.94 us -> 3.14 us
where the time goes in v2:
time: 72.8 us; the launch traced here: 71.9 us
  Pallas kernels  68.1 us (94%)
  local copies, waits for them, and re-layouts  3.14 us (4%)
    pallas_call x1, Pallas kernels, on_device(): pl.pallas_call(kernel, out_shape=(out, out), in_specs=[pl.BlockSpec(memor...  68.1 us
    unnamed x2, local copies, waits for them, and re-layouts  3.14 us

profile of v2, /device:TPU:1, one launch (start us, length us, event | category | flops | bytes accessed | tf_op | source)
XLA Modules:
  0.0 71.9 jit_solution(8707232395531651201)
XLA Ops:
  0.6 68.1 %shard_map.50 = (f32[8,32,128]{2,1,0:T(8,128)}, f32[8,32,128]{2,1,0:T(8,128)}) custom-call(f32[8,2,2,128,128]{4,3,2,1,0:T(8,128)} %bitcast.2, f32[8,128,128]{2,1,0:T(8,128)} %u_hbm.1, f32[8,2,2,128,128]{4,3,2,1,0:T(8,128)} %bitcast.3), custom_call_target="tpu_custom_call" | custom-call | tf_op jit(solution)/shard_map/pallas_call | solution.py:487
  68.8 1.6 %copy.7 = f32[8,32,128]{2,1,0:T(8,128)} copy(f32[8,32,128]{2,1,0:T(8,128)} %get-tuple-element.4) | data formatting | bytes 262144
  70.3 1.6 %copy.8 = f32[8,32,128]{2,1,0:T(8,128)} copy(f32[8,32,128]{2,1,0:T(8,128)} %get-tuple-element.5) | data formatting | bytes 262144

commit v3 on v2

--- a/solution.py
+++ b/solution.py
@@ -14,6 +14,7 @@
 S = 8
 ROWS = 32
 NX, NY = 4, 4
+EARLY = 3
 
 
 def split(a):
@@ -76,9 +77,10 @@
 def kernel(
     g_hbm, u_hbm, c_hbm, on_ref, cp_ref,
     g, u, c, link, pre, own, tbuf, xs, ys, ex, ey, lp, lo, zbuf, dbuf, zrecv, xin,
-    ap, gt, w0, q, gg, vv, xt, w, part, relay, recv,
+    ap, maps, w0, q, gg, vv, xt, w,
+    stage, up, down_rows, mid, kept, from_below, from_above, passed,
     g_sem, in_sem, pair_sem, x_send, x_recv, y_send, y_recv, z_sem, d_sem, h_sem,
-    r_send, r_recv,
+    r_send, r_recv, p_send, p_recv,
 ):
     s = lax.axis_index("slab")
     e = lax.axis_index("energy")
@@ -130,27 +132,25 @@
     def cat(ref, i, k):
         return jnp.concatenate([ref[i, k, 0], ref[i, k, 1]], 1)
 
-    def flip(i):
-        for k in range(2):
-            gt[i, k] = jnp.concatenate([g[i, k, 0].T, g[i, k, 1].T], 1)
-
     g_copy(0).wait()
-    flip(0)
     for k in range(2):
-        pre[0, k] = gt[0, k]
+        pre[0, k] = jnp.concatenate([g[0, k, 0].T, g[0, k, 1].T], 1)
     cu.wait()
 
-    def chain(i, carry):
+    def make_link(i):
         g_copy(i + 1).wait()
         uu = lhs(u[i])
         for k in range(2):
             gh, gl = split(jnp.concatenate([g[i + 1, k, 0], g[i + 1, k, 1]], 0))
-            value = mul(uu, (gh, gl), True)
-            link[i, k] = value
-            pre[i + 1, k] = mul(lhs(pre[i, k]), rhs(value))
-        return carry
-
-    lax.fori_loop(0, S - 1, chain, 0)
+            link[i, k] = mul(uu, (gh, gl), True)
+
+    make_link(0)
+    make_link(1)
+    for i in range(S - 1):
+        for k in range(2):
+            pre[i + 1, k] = mul(lhs(pre[i, k]), rhs(link[i, k]))
+        if i < S - 3:
+            make_link(i + 2)
     last_u = u[S - 1] * jnp.where(last, 0.0, 1.0).astype(F32)
     uw = split(last_u)
     for k in range(2):
@@ -172,11 +172,15 @@
     for k in range(2):
         own[k, 0] = jnp.zeros((B, 2 * B), F32)
 
-    def fold(i, carry):
+    def fold(n, carry):
         for k in range(2):
-            pk = pre[i, k]
-            yk = mul(lhs(pk), rhs(cat(c, i, k)))
-            own[k, 0] += mul(lhs(yk), rhs_t(pk), True)
+            total = own[k, 0]
+            for m in range(2):
+                i = 2 * n + m
+                pk = pre[i, k]
+                yk = mul(lhs(pk), rhs(cat(c, i, k)))
+                total += mul(lhs(yk), rhs_t(pk), True)
+            own[k, 0] = total
         return carry
 
     class Ring:
@@ -223,12 +227,12 @@
     def prod(p1, p2):
         return mul(lhs(p1), rhs(p2))
 
-    FOLD_CUT = 4
-    lax.fori_loop(0, FOLD_CUT, fold, 0)
+    lax.fori_loop(0, 1, fold, 0)
     pair(1).wait_recv()
     xs[x, 1] = prod(tbuf[0, 1], tbuf[1, 1])
     xp.start()
-    lax.fori_loop(FOLD_CUT, S, fold, 0)
+
+    lax.fori_loop(1, S // 2, fold, 0)
     pair(0).start()
     tbuf[core, 0] = own[core, 0]
     xp.forward()
@@ -236,42 +240,39 @@
     xs[x, 0] = apply_map(tbuf[0, 0], tbuf[0, 1], tbuf[1, 0])
     xo.start()
 
-    def prepare(i):
-        flip(i)
+    def prepare(i, k):
         uh, ul = split(u[i])
         uu = jnp.concatenate([uh, ul], 1)
-        for k in range(2):
-            a0, ps = ap[k, 0], ap[k, 1]
-            gi, gti = cat(g, i, k), gt[i, k]
-            lg = lhs(gi)
-            lt = lhs(gti)
-            h0 = mul(lt, rhs(a0))
-            w0[i, k] = mul(lhs(h0), rhs(gti))
-            pw = rhs(ps)
-            q[i, k] = lhs(mul(lt, pw))
-            gg[i, k] = mul(lg, pw)
-            rows = [gi[:, :B], -gi[:, B:], gti[:, :B], -gti[:, B:]]
-            xh, xl = split(jnp.concatenate(rows, 0))
-            t = dot(xh, uu)
-            vh, vl = split(t[:, :B] + t[:, B:] + dot(xl, uh))
-            for n in range(4):
-                column = (n // 2) * 512 + k * 256 + (n % 2) * B
-                vv[i, 0:B, column : column + B] = vh[n * B : n * B + B]
-                vv[i, B : 2 * B, column : column + B] = vl[n * B : n * B + B]
-
-    def step_back(i):
-        for k in range(2):
-            lk = link[i, k]
-            left = lhs(lk)
-            yk = mul(left, rhs(ap[k, 0]))
-            pk = mul(left, rhs(ap[k, 1]))
-            ap[k, 1] = pk
-            ap[k, 0] = cat(c, i, k) + mul(lhs(yk), rhs_t(lk), True)
+        gi = cat(g, i, k)
+        gti = jnp.concatenate([g[i, k, 0].T, g[i, k, 1].T], 1)
+        lg = lhs(gi)
+        lt = lhs(gti)
+        h0 = mul(lt, rhs(ap[i, k, 0]))
+        pw = rhs(ap[i, k, 1])
+        q[i, k] = lhs(mul(lt, pw))
+        gg[i, k] = mul(lg, pw)
+        w0[i, k] = mul(lhs(h0), rhs(gti))
+        rows = [gi[:, :B], -gi[:, B:], gti[:, :B], -gti[:, B:]]
+        xh, xl = split(jnp.concatenate(rows, 0))
+        t = dot(xh, uu)
+        vh, vl = split(t[:, :B] + t[:, B:] + dot(xl, uh))
+        for n in range(4):
+            row = n * B
+            column = (n % 2) * B
+            vv[i, k, n // 2, 0:B, column : column + B] = vh[row : row + B]
+            vv[i, k, n // 2, B : 2 * B, column : column + B] = vl[row : row + B]
+
+    def step_back(i, k):
+        lk = link[i, k]
+        left = lhs(lk)
+        yk = mul(left, rhs(ap[i + 1, k, 0]))
+        ap[i, k, 1] = mul(left, rhs(ap[i + 1, k, 1]))
+        ap[i, k, 0] = cat(c, i, k) + mul(lhs(yk), rhs_t(lk), True)
 
     zero = jnp.zeros((B, 2 * B), F32)
     for k in range(2):
-        ap[k, 0] = cat(c, S - 1, k)
-        ap[k, 1] = jnp.concatenate([last_u, jnp.zeros((B, B), F32)], 1)
+        ap[S - 1, k, 0] = cat(c, S - 1, k)
+        ap[S - 1, k, 1] = jnp.concatenate([last_u, jnp.zeros((B, B), F32)], 1)
 
     def level_p(ref, n):
         lp[n, 0] = prod(ref[0, 1], ref[1, 1])
@@ -300,30 +301,30 @@
     zcopy = remote(zbuf, zrecv, z_sem.at[0], z_sem.at[1], (zpeer, e))
 
     def shadow(j, carry):
-        i = S - 1 - j
-
-        @pl.when(j > 0)
-        def _():
-            step_back(i)
-
-        prepare(i)
-
-        @pl.when(j == 0)
+        i = S - 1 - j // 2
+        k = lax.rem(j, 2)
+        step_back(i, k)
+
+        @pl.when(i < EARLY)
+        def _():
+            prepare(i, k)
+
+        @pl.when(j == 4)
         def _():
             xp.finish()
             level_p(xs, 0)
             ys[y, 1] = prod(lp[0, 0], lp[0, 1])
             yp.start()
 
-        @pl.when(j == 1)
+        @pl.when(j == 5)
         def _():
             xo.forward()
 
-        @pl.when(j == 2)
+        @pl.when(j == 8)
         def _():
             yp.forward()
 
-        @pl.when(j == 3)
+        @pl.when(j == 10)
         def _():
             xo.finish()
             ys[y, 0] = level_o(xs, 0)
@@ -331,130 +332,166 @@
             yp.finish()
             level_p(ys, 1)
 
-        @pl.when(j == 4)
+        @pl.when(j == 12)
         def _():
             yo.forward()
             later(xs, ex, 0)
-
-        @pl.when(j == 6)
-        def _():
-            yo.finish()
-            zbuf[...] = level_o(ys, 1)
-
-            @pl.when(z == 1)
-            def _():
-                zcopy.start()
-                zrecv[...] = zero
+            o, p = combine((tbuf[1, 0], tbuf[1, 1]), (ex[x, 0], ex[x, 1]))
+            maps[0, 0] = ex[x, 0]
+            maps[0, 1] = ex[x, 1]
+            maps[1, 0] = o
+            maps[1, 1] = p
 
         return carry
 
-    lax.fori_loop(0, S, shadow, 0)
+    lax.fori_loop(2, 2 * S, shadow, 0)
+    yo.finish()
+    zbuf[...] = level_o(ys, 1)
+
+    @pl.when(z == 1)
+    def _():
+        zcopy.start()
 
     later(ys, ey, 1)
-    outer = combine((ex[x, 0], ex[x, 1]), (ey[y, 0], ey[y, 1]))
-    inner = combine((tbuf[1, 0], tbuf[1, 1]), outer)
+    outer_y = (ey[y, 0], ey[y, 1])
+    for n in range(2):
+        o, p = combine((maps[n, 0], maps[n, 1]), outer_y)
+        maps[n, 0] = o
+        maps[n, 1] = p
+
+    give, keep = core, 1 - core
+
+    @pl.when(z == 1)
+    def _():
+        dbuf[...] = maps[give, 0]
+        xin[core] = maps[keep, 0]
 
     @pl.when(z == 0)
     def _():
+        for k in range(2):
+            prepare(EARLY, k)
         zcopy.wait_recv()
-
-    top = zrecv[...]
-    chip_in = apply_map(outer[0], outer[1], top)
-    core_in = apply_map(inner[0], inner[1], top)
-    is_first = core == 0
-    dbuf[...] = jnp.where(is_first, chip_in, core_in)
+        dbuf[...] = apply_map(maps[give, 0], maps[give, 1], zrecv[...])
+
     down = remote(dbuf, xin.at[core], d_sem.at[0], d_sem.at[1], (partner, e))
     down.start()
-    xin[core] = jnp.where(is_first, core_in, chip_in)
-    down.wait_recv()
-
-    for k in range(2):
+
+    @pl.when(z == 0)
+    def _():
+        xin[core] = apply_map(maps[keep, 0], maps[keep, 1], zrecv[...])
+
+    def weigh(i, k):
+        zk = mul(q[i, k], (xt[k, 0], xt[k, 1]))
+        w[i, k] = w0[i, k] + mul(lhs(zk), rhs_t(gg[i, k]), True)
+
+    def first_weights(n, carry):
+        k = jnp.where(n == 0, core, 1 - core)
+
+        @pl.when(n == 1)
+        def _():
+            down.wait_recv()
+
         high, low = rhs(xin[k])
         xt[k, 0] = high
         xt[k, 1] = low
-
-    def weights(i):
-        for k in range(2):
-            zk = mul(q[i, k], (xt[k, 0], xt[k, 1]))
-            w[i, k] = w0[i, k] + mul(lhs(zk), rhs_t(gg[i, k]), True)
-
-    weights(0)
+        weigh(0, k)
+        return carry
+
+    lax.fori_loop(0, 2, first_weights, 0)
     halo = remote(w.at[0], w.at[S], h_sem.at[0], h_sem.at[1], (prev, e))
-    halo.start()
+
+    @pl.when(s > 0)
+    def _():
+        halo.start()
+
+    ready = EARLY + 1 - z
 
     def spread(i, n):
-        step = (3, 1, 1, 3)[n]
-        kind = (0, 1, 0, 1)[n]
-        owner = epeer(2) if n < 2 else epeer(step)
-        target = relay.at[i, kind] if n < 2 else recv.at[i, 0, kind]
         return remote(
-            part.at[i, owner, kind], target,
-            r_send.at[i, n], r_recv.at[i, n], (s, epeer(step)),
+            (up, down_rows)[n].at[i], (from_below, from_above)[n].at[i],
+            r_send.at[i, n], r_recv.at[i, n], (s, epeer((1, 3)[n])),
         )
 
-    def pass_on(i, kind):
-        step = (3, 1)[kind]
+    def pass_on(pair_no, kind):
+        at = pl.ds(2 * pair_no, 2)
         return remote(
-            relay.at[i, kind], recv.at[i, 1, kind],
-            r_send.at[i, 4 + kind], r_recv.at[i, 4 + kind], (s, epeer(step)),
+            mid.at[kind, at], passed.at[kind, at],
+            p_send.at[pair_no, kind], p_recv.at[pair_no, kind], (s, epeer((3, 1)[kind])),
         )
 
+    def rows_of(kind, d):
+        return stage[kind, pl.ds(pl.multiple_of(epeer(d) * ROWS, ROWS), ROWS)]
+
+    def pass_step(pair_no, carry):
+        for m in range(2):
+            i = 2 * pair_no + m
+            for n in range(2):
+                spread(i, n).wait_recv()
+            mid[0, i] += from_above[i, 0]
+            mid[1, i] += from_below[i, 1]
+        for kind in range(2):
+            pass_on(pair_no, kind).start()
+        return carry
+
     def finals(i, carry):
+        stage[0] = w[i, 0, :, 0:B] + w[i, 1, :, 0:B]
+
+        @pl.when((i < S - 1) & (i + 1 >= ready))
+        def _():
+            for k in range(2):
+                prepare(i + 1, k)
+
         @pl.when(i < S - 1)
         def _():
-            weights(i + 1)
+            for k in range(2):
+                weigh(i + 1, k)
 
         @pl.when(i == S - 1)
         def _():
-            halo.wait_recv()
+            @pl.when(s < slabs - 1)
+            def _():
+                halo.wait_recv()
 
             @pl.when(last)
             def _():
                 for k in range(2):
                     w[S, k] = zero
 
-        wh0, wl0 = split(w[i + 1, 0])
-        wh1, wl1 = split(w[i + 1, 1])
-        nt = jnp.concatenate(
-            [jnp.concatenate([wh0, wh1], 1), jnp.concatenate([wl0, wl1], 1)], 0
-        )
-        nn = jnp.concatenate(
-            [
-                jnp.concatenate([h[:, m : m + B], l[:, m : m + B]], 1)
-                for h, l in ((wh0, wl0), (wh1, wl1))
-                for m in (0, B)
-            ],
-            0,
-        )
-        t = dot(vv[i, :, 0:512], nt, True) + dot(vv[i, :, 512:1024], nn)
-        coupling = t[:B, :B] + (t[:B, B:] + t[B:, :B])
-        onsite = w[i, 0, :, 0:B] + w[i, 1, :, 0:B]
-        for r in range(4):
-            part[i, r, 0] = onsite[r * ROWS : (r + 1) * ROWS]
-            part[i, r, 1] = coupling[r * ROWS : (r + 1) * ROWS]
-        for n in range(4):
+        t = None
+        for k in range(2):
+            wh, wl = split(w[i + 1, k])
+            nt = jnp.concatenate([wh, wl], 0)
+            nn = jnp.concatenate(
+                [jnp.concatenate([wh[:, m : m + B], wl[:, m : m + B]], 1) for m in (0, B)], 0
+            )
+            tk = dot(vv[i, k, 0], nt, True) + dot(vv[i, k, 1], nn)
+            t = tk if t is None else t + tk
+        stage[1] = t[:B, :B] + (t[:B, B:] + t[B:, :B])
+        up[i, 0] = rows_of(0, 1)
+        up[i, 1] = rows_of(1, 2)
+        down_rows[i, 0] = rows_of(0, 2)
+        down_rows[i, 1] = rows_of(1, 3)
+        for n in range(2):
             spread(i, n).start()
+        mid[0, i] = rows_of(0, 3)
+        mid[1, i] = rows_of(1, 1)
+        for kind in range(2):
+            kept[i, kind] = rows_of(kind, 0)
         return carry
 
     lax.fori_loop(0, S, finals, 0)
-
-    def pass_all(i, carry):
-        for kind, step in ((0, 3), (1, 1)):
-            spread(i, kind).wait_recv()
-            relay[i, kind] += part[i, epeer(step), kind]
-            pass_on(i, kind).start()
+    lax.fori_loop(0, S // 2, pass_step, 0)
+
+    def collect(pair_no, carry):
+        for kind in range(2):
+            pass_on(pair_no, kind).wait_recv()
+        for m in range(2):
+            i = 2 * pair_no + m
+            on_ref[i] = kept[i, 0] + from_below[i, 0] + passed[0, i]
+            cp_ref[i] = kept[i, 1] + from_above[i, 1] + passed[1, i]
         return carry
 
-    lax.fori_loop(0, S, pass_all, 0)
-
-    def collect(i, carry):
-        for kind, out in ((0, on_ref), (1, cp_ref)):
-            spread(i, 2 + kind).wait_recv()
-            pass_on(i, kind).wait_recv()
-            out[i] = part[i, e, kind] + recv[i, 0, kind] + recv[i, 1, kind]
-        return carry
-
-    lax.fori_loop(0, S, collect, 0)
+    lax.fori_loop(0, S // 2, collect, 0)
 
     for t in range(2):
         pair(t).wait_send()
@@ -466,16 +503,19 @@
         zcopy.wait_send()
 
     down.wait_send()
-    halo.wait_send()
+
+    @pl.when(s > 0)
+    def _():
+        halo.wait_send()
 
     def drain(i, carry):
-        for n in range(4):
-            spread(i, n).wait_send()
-        for kind in range(2):
-            pass_on(i, kind).wait_send()
+        for n in range(2):
+            spread(2 * i, n).wait_send()
+            spread(2 * i + 1, n).wait_send()
+            pass_on(i, n).wait_send()
         return carry
 
-    lax.fori_loop(0, S, drain, 0)
+    lax.fori_loop(0, S // 2, drain, 0)
 
 
 def on_device(green_blocks, couplings, green_cotangent):
@@ -507,17 +547,22 @@
             vmem(block, F32),
             vmem(block, F32),
             vmem((2,) + block, F32),
+            vmem((S, 2, 2) + block, F32),
             vmem((2, 2) + block, F32),
-            vmem((S, 2) + block, F32),
             vmem((S, 2) + block, F32),
             vmem((S, 2, 2 * B, 2 * B), BF16),
             vmem((S, 2) + block, F32),
-            vmem((S, 2 * B, 8 * B), BF16),
+            vmem((S, 2, 2, 2 * B, 2 * B), BF16),
             vmem((2, 2, 2 * B, 2 * B), BF16),
             vmem((S + 1, 2) + block, F32),
-            vmem((S, 4, 2, ROWS, B), F32),
+            vmem((2, B, B), F32),
             vmem((S, 2, ROWS, B), F32),
-            vmem((S, 2, 2, ROWS, B), F32),
+            vmem((S, 2, ROWS, B), F32),
+            vmem((2, S, ROWS, B), F32),
+            vmem((S, 2, ROWS, B), F32),
+            vmem((S, 2, ROWS, B), F32),
+            vmem((S, 2, ROWS, B), F32),
+            vmem((2, S, ROWS, B), F32),
             dma((S,)),
             dma((2,)),
             dma((2, 2)),
@@ -528,8 +573,10 @@
             dma((2,)),
             dma((2,)),
             dma((2,)),
-            dma((S, 6)),
-            dma((S, 6)),
+            dma((S, 2)),
+            dma((S, 2)),
+            dma((S // 2, 2)),
+            dma((S // 2, 2)),
         ],
         compiler_params=pltpu.CompilerParams(
             collective_id=0, has_side_effects=True, vmem_limit_bytes=62 * 1024 * 1024

time: 72.8 us -> 70.2 us (0.964); the launches traced: 71.9 us -> 70 us
  Pallas kernels: 68.1 us -> 66.3 us
    pallas_call x1, Pallas kernels: 68.1 us -> 66.3 us  [on_device(): pl.pallas_call(kernel, out_shape=(out, out), in_specs=[pl.BlockSpec(memor...]
where the time goes in v3:
time: 70.2 us; the launch traced here: 70 us
  Pallas kernels  66.3 us (94%)
  local copies, waits for them, and re-layouts  3.14 us (4%)
    pallas_call x1, Pallas kernels, on_device(): pl.pallas_call(kernel, out_shape=(out, out), in_specs=[pl.BlockSpec(memor...  66.3 us
    unnamed x2, local copies, waits for them, and re-layouts  3.14 us

profile of v3, /device:TPU:1, one launch (start us, length us, event | category | flops | bytes accessed | tf_op | source)
XLA Modules:
  0.0 70.0 jit_solution(5629845182098607918)
XLA Ops:
  0.6 66.3 %shard_map.50 = (f32[8,32,128]{2,1,0:T(8,128)}, f32[8,32,128]{2,1,0:T(8,128)}) custom-call(f32[8,2,2,128,128]{4,3,2,1,0:T(8,128)} %bitcast.2, f32[8,128,128]{2,1,0:T(8,128)} %u_hbm.1, f32[8,2,2,128,128]{4,3,2,1,0:T(8,128)} %bitcast.3), custom_call_target="tpu_custom_call" | custom-call | tf_op jit(solution)/shard_map/pallas_call | solution.py:527
  66.9 1.6 %copy.7 = f32[8,32,128]{2,1,0:T(8,128)} copy(f32[8,32,128]{2,1,0:T(8,128)} %get-tuple-element.4) | data formatting | bytes 262144
  68.5 1.6 %copy.8 = f32[8,32,128]{2,1,0:T(8,128)} copy(f32[8,32,128]{2,1,0:T(8,128)} %get-tuple-element.5) | data formatting | bytes 262144

commit v4 on v3

--- a/solution.py
+++ b/solution.py
@@ -14,7 +14,7 @@
 S = 8
 ROWS = 32
 NX, NY = 4, 4
-EARLY = 3
+EARLY = 6
 
 
 def split(a):
@@ -76,7 +76,7 @@
 
 def kernel(
     g_hbm, u_hbm, c_hbm, on_ref, cp_ref,
-    g, u, c, link, pre, own, tbuf, xs, ys, ex, ey, lp, lo, zbuf, dbuf, zrecv, xin,
+    g, u, c, link, head, own, tbuf, xs, ys, ex, ey, lp, lo, zbuf, dbuf, zrecv, xin,
     ap, maps, w0, q, gg, vv, xt, w,
     stage, up, down_rows, mid, kept, from_below, from_above, passed,
     g_sem, in_sem, pair_sem, x_send, x_recv, y_send, y_recv, z_sem, d_sem, h_sem,
@@ -117,9 +117,9 @@
 
     cu = pltpu.make_async_copy(u_hbm, u, in_sem.at[0])
     cc = pltpu.make_async_copy(c_hbm, c, in_sem.at[1])
-    g_copy(0).start()
+    g_copy(S - 1).start()
     cu.start()
-    for i in range(1, S):
+    for i in range(S - 2, -1, -1):
         g_copy(i).start()
     cc.start()
 
@@ -132,31 +132,29 @@
     def cat(ref, i, k):
         return jnp.concatenate([ref[i, k, 0], ref[i, k, 1]], 1)
 
-    g_copy(0).wait()
+    cu.wait()
+    g_copy(S - 1).wait()
+    last_u = u[S - 1] * jnp.where(last, 0.0, 1.0).astype(F32)
     for k in range(2):
-        pre[0, k] = jnp.concatenate([g[0, k, 0].T, g[0, k, 1].T], 1)
-    cu.wait()
+        ap[S - 1, k, 1] = jnp.concatenate([last_u, jnp.zeros((B, B), F32)], 1)
 
     def make_link(i):
-        g_copy(i + 1).wait()
         uu = lhs(u[i])
         for k in range(2):
             gh, gl = split(jnp.concatenate([g[i + 1, k, 0], g[i + 1, k, 1]], 0))
             link[i, k] = mul(uu, (gh, gl), True)
-
-    make_link(0)
-    make_link(1)
-    for i in range(S - 1):
+        g_copy(i).wait()
+
+    make_link(S - 2)
+    make_link(S - 3)
+    for i in range(S - 2, -1, -1):
         for k in range(2):
-            pre[i + 1, k] = mul(lhs(pre[i, k]), rhs(link[i, k]))
-        if i < S - 3:
-            make_link(i + 2)
-    last_u = u[S - 1] * jnp.where(last, 0.0, 1.0).astype(F32)
-    uw = split(last_u)
+            ap[i, k, 1] = mul(lhs(link[i, k]), rhs(ap[i + 1, k, 1]))
+        if i > 1:
+            make_link(i - 2)
     for k in range(2):
-        value = pre[S - 1, k]
-        t = mul(lhs(jnp.concatenate([value[:, :B], value[:, B:]], 0)), uw)
-        own[k, 1] = jnp.concatenate([t[:B], t[B:]], 1)
+        head[k] = jnp.concatenate([g[0, k, 0].T, g[0, k, 1].T], 1)
+        own[k, 1] = mul(lhs(head[k]), rhs(ap[0, k, 1]))
 
     pl.semaphore_wait(barrier, len(greet))
 
@@ -170,18 +168,13 @@
     tbuf[core, 1] = own[core, 1]
     cc.wait()
     for k in range(2):
-        own[k, 0] = jnp.zeros((B, 2 * B), F32)
-
-    def fold(n, carry):
+        ap[S - 1, k, 0] = cat(c, S - 1, k)
+
+    def fold(i):
+        lk = [link[i, k] for k in range(2)]
+        half = [mul(lhs(lk[k]), rhs(ap[i + 1, k, 0])) for k in range(2)]
         for k in range(2):
-            total = own[k, 0]
-            for m in range(2):
-                i = 2 * n + m
-                pk = pre[i, k]
-                yk = mul(lhs(pk), rhs(cat(c, i, k)))
-                total += mul(lhs(yk), rhs_t(pk), True)
-            own[k, 0] = total
-        return carry
+            ap[i, k, 0] = cat(c, i, k) + mul(lhs(half[k]), rhs_t(lk[k]), True)
 
     class Ring:
         def __init__(self, ref, t, me, peer, send, recv_):
@@ -227,12 +220,17 @@
     def prod(p1, p2):
         return mul(lhs(p1), rhs(p2))
 
-    lax.fori_loop(0, 1, fold, 0)
+    for i in range(S - 2, S - 5, -1):
+        fold(i)
     pair(1).wait_recv()
     xs[x, 1] = prod(tbuf[0, 1], tbuf[1, 1])
     xp.start()
 
-    lax.fori_loop(1, S // 2, fold, 0)
+    for i in range(S - 5, -1, -1):
+        fold(i)
+    half = [mul(lhs(head[k]), rhs(ap[0, k, 0])) for k in range(2)]
+    for k in range(2):
+        own[k, 0] = mul(lhs(half[k]), rhs_t(head[k]), True)
     pair(0).start()
     tbuf[core, 0] = own[core, 0]
     xp.forward()
@@ -240,47 +238,42 @@
     xs[x, 0] = apply_map(tbuf[0, 0], tbuf[0, 1], tbuf[1, 0])
     xo.start()
 
-    def prepare(i, k):
+    def prepare(i):
         uh, ul = split(u[i])
         uu = jnp.concatenate([uh, ul], 1)
-        gi = cat(g, i, k)
-        gti = jnp.concatenate([g[i, k, 0].T, g[i, k, 1].T], 1)
-        lg = lhs(gi)
-        lt = lhs(gti)
-        h0 = mul(lt, rhs(ap[i, k, 0]))
-        pw = rhs(ap[i, k, 1])
-        q[i, k] = lhs(mul(lt, pw))
-        gg[i, k] = mul(lg, pw)
-        w0[i, k] = mul(lhs(h0), rhs(gti))
-        rows = [gi[:, :B], -gi[:, B:], gti[:, :B], -gti[:, B:]]
-        xh, xl = split(jnp.concatenate(rows, 0))
-        t = dot(xh, uu)
-        vh, vl = split(t[:, :B] + t[:, B:] + dot(xl, uh))
-        for n in range(4):
-            row = n * B
-            column = (n % 2) * B
-            vv[i, k, n // 2, 0:B, column : column + B] = vh[row : row + B]
-            vv[i, k, n // 2, B : 2 * B, column : column + B] = vl[row : row + B]
-
-    def step_back(i, k):
-        lk = link[i, k]
-        left = lhs(lk)
-        yk = mul(left, rhs(ap[i + 1, k, 0]))
-        ap[i, k, 1] = mul(left, rhs(ap[i + 1, k, 1]))
-        ap[i, k, 0] = cat(c, i, k) + mul(lhs(yk), rhs_t(lk), True)
+        ks = range(2)
+        gi = [cat(g, i, k) for k in ks]
+        gti = [jnp.concatenate([g[i, k, 0].T, g[i, k, 1].T], 1) for k in ks]
+        lt = [lhs(gti[k]) for k in ks]
+        h0 = [mul(lt[k], rhs(ap[i, k, 0])) for k in ks]
+        for k in ks:
+            pw = rhs(ap[i, k, 1])
+            q[i, k] = lhs(mul(lt[k], pw))
+            gg[i, k] = mul(lhs(gi[k]), pw)
+        for k in ks:
+            w0[i, k] = mul(lhs(h0[k]), rhs(gti[k]))
+        for k in ks:
+            rows = [gi[k][:, :B], -gi[k][:, B:], gti[k][:, :B], -gti[k][:, B:]]
+            xh, xl = split(jnp.concatenate(rows, 0))
+            t = dot(xh, uu)
+            vh, vl = split(t[:, :B] + t[:, B:] + dot(xl, uh))
+            for n in range(4):
+                row = n * B
+                column = (n % 2) * B
+                vv[i, n // 2, k, 0:B, column : column + B] = vh[row : row + B]
+                vv[i, n // 2, k, B : 2 * B, column : column + B] = vl[row : row + B]
 
     zero = jnp.zeros((B, 2 * B), F32)
-    for k in range(2):
-        ap[S - 1, k, 0] = cat(c, S - 1, k)
-        ap[S - 1, k, 1] = jnp.concatenate([last_u, jnp.zeros((B, B), F32)], 1)
 
     def level_p(ref, n):
         lp[n, 0] = prod(ref[0, 1], ref[1, 1])
         lp[n, 1] = prod(ref[2, 1], ref[3, 1])
 
     def level_o(ref, n):
-        o01 = apply_map(ref[0, 0], ref[0, 1], ref[1, 0])
-        o23 = apply_map(ref[2, 0], ref[2, 1], ref[3, 0])
+        half = [mul(lhs(ref[m, 1]), rhs(ref[m + 1, 0])) for m in (2, 0)]
+        o23, o01 = [
+            ref[m, 0] + mul(lhs(h), rhs_t(ref[m, 1]), True) for m, h in zip((2, 0), half)
+        ]
         lo[n] = o23
         return apply_map(o01, lp[n, 0], o23)
 
@@ -300,51 +293,30 @@
 
     zcopy = remote(zbuf, zrecv, z_sem.at[0], z_sem.at[1], (zpeer, e))
 
-    def shadow(j, carry):
-        i = S - 1 - j // 2
-        k = lax.rem(j, 2)
-        step_back(i, k)
-
-        @pl.when(i < EARLY)
-        def _():
-            prepare(i, k)
-
-        @pl.when(j == 4)
-        def _():
-            xp.finish()
-            level_p(xs, 0)
-            ys[y, 1] = prod(lp[0, 0], lp[0, 1])
-            yp.start()
-
-        @pl.when(j == 5)
-        def _():
-            xo.forward()
-
-        @pl.when(j == 8)
-        def _():
-            yp.forward()
-
-        @pl.when(j == 10)
-        def _():
-            xo.finish()
-            ys[y, 0] = level_o(xs, 0)
-            yo.start()
-            yp.finish()
-            level_p(ys, 1)
-
-        @pl.when(j == 12)
-        def _():
-            yo.forward()
-            later(xs, ex, 0)
-            o, p = combine((tbuf[1, 0], tbuf[1, 1]), (ex[x, 0], ex[x, 1]))
-            maps[0, 0] = ex[x, 0]
-            maps[0, 1] = ex[x, 1]
-            maps[1, 0] = o
-            maps[1, 1] = p
-
-        return carry
-
-    lax.fori_loop(2, 2 * S, shadow, 0)
+    prepare(0)
+    xp.finish()
+    level_p(xs, 0)
+    ys[y, 1] = prod(lp[0, 0], lp[0, 1])
+    yp.start()
+    prepare(1)
+    xo.forward()
+    prepare(2)
+    yp.forward()
+    prepare(3)
+    xo.finish()
+    ys[y, 0] = level_o(xs, 0)
+    yo.start()
+    yp.finish()
+    level_p(ys, 1)
+    later(xs, ex, 0)
+    o, p = combine((tbuf[1, 0], tbuf[1, 1]), (ex[x, 0], ex[x, 1]))
+    maps[0, 0] = ex[x, 0]
+    maps[0, 1] = ex[x, 1]
+    maps[1, 0] = o
+    maps[1, 1] = p
+    yo.forward()
+    for i in range(4, EARLY):
+        prepare(i)
     yo.finish()
     zbuf[...] = level_o(ys, 1)
 
@@ -354,10 +326,15 @@
 
     later(ys, ey, 1)
     outer_y = (ey[y, 0], ey[y, 1])
+    ly = [lhs(maps[n, 1]) for n in range(2)]
+    half = [mul(ly[n], rhs(ey[y, 0])) for n in range(2)]
+    prods = [mul(ly[n], rhs(ey[y, 1])) for n in range(2)]
+    offs = [
+        maps[n, 0] + mul(lhs(half[n]), rhs_t(maps[n, 1]), True) for n in range(2)
+    ]
     for n in range(2):
-        o, p = combine((maps[n, 0], maps[n, 1]), outer_y)
-        maps[n, 0] = o
-        maps[n, 1] = p
+        maps[n, 0] = offs[n]
+        maps[n, 1] = prods[n]
 
     give, keep = core, 1 - core
 
@@ -368,8 +345,7 @@
 
     @pl.when(z == 0)
     def _():
-        for k in range(2):
-            prepare(EARLY, k)
+        prepare(EARLY)
         zcopy.wait_recv()
         dbuf[...] = apply_map(maps[give, 0], maps[give, 1], zrecv[...])
 
@@ -438,13 +414,13 @@
 
         @pl.when((i < S - 1) & (i + 1 >= ready))
         def _():
-            for k in range(2):
-                prepare(i + 1, k)
+            prepare(i + 1)
 
         @pl.when(i < S - 1)
         def _():
+            zs = [mul(q[i + 1, k], (xt[k, 0], xt[k, 1])) for k in range(2)]
             for k in range(2):
-                weigh(i + 1, k)
+                w[i + 1, k] = w0[i + 1, k] + mul(lhs(zs[k]), rhs_t(gg[i + 1, k]), True)
 
         @pl.when(i == S - 1)
         def _():
@@ -457,15 +433,15 @@
                 for k in range(2):
                     w[S, k] = zero
 
-        t = None
+        nts, nns = [], []
         for k in range(2):
             wh, wl = split(w[i + 1, k])
-            nt = jnp.concatenate([wh, wl], 0)
-            nn = jnp.concatenate(
-                [jnp.concatenate([wh[:, m : m + B], wl[:, m : m + B]], 1) for m in (0, B)], 0
-            )
-            tk = dot(vv[i, k, 0], nt, True) + dot(vv[i, k, 1], nn)
-            t = tk if t is None else t + tk
+            nts.append(jnp.concatenate([wh, wl], 0))
+            for m in (0, B):
+                nns.append(jnp.concatenate([wh[:, m : m + B], wl[:, m : m + B]], 1))
+        t = dot(
+            jnp.concatenate([vv[i, 0, 0], vv[i, 0, 1]], 1), jnp.concatenate(nts, 1), True
+        ) + dot(jnp.concatenate([vv[i, 1, 0], vv[i, 1, 1]], 1), jnp.concatenate(nns, 0))
         stage[1] = t[:B, :B] + (t[:B, B:] + t[B:, :B])
         up[i, 0] = rows_of(0, 1)
         up[i, 1] = rows_of(1, 2)
@@ -534,7 +510,7 @@
             vmem((S, B, B), F32),
             vmem(shape, F32),
             vmem((S, 2) + block, F32),
-            vmem((S, 2) + block, F32),
+            vmem((2,) + block, F32),
             vmem((2, 2) + block, F32),
             vmem((2, 2) + block, F32),
             vmem((NX, 2) + block, F32),

time: 70.2 us -> 66.6 us (0.949)
  Pallas kernels: 66.3 us -> 62.7 us
    pallas_call x1, Pallas kernels: 66.3 us -> 62.7 us  [on_device(): pl.pallas_call(kernel, out_shape=(out, out), in_specs=[pl.BlockSpec(memor...]
where the time goes in v4:
time: 66.6 us; the launch traced here: 66.5 us
  Pallas kernels  62.7 us (94%)
  local copies, waits for them, and re-layouts  3.14 us (5%)
    pallas_call x1, Pallas kernels, on_device(): pl.pallas_call(kernel, out_shape=(out, out), in_specs=[pl.BlockSpec(memor...  62.7 us
    unnamed x2, local copies, waits for them, and re-layouts  3.14 us

profile of v4, /device:TPU:1, one launch (start us, length us, event | category | flops | bytes accessed | tf_op | source)
XLA Modules:
  0.0 66.5 jit_solution(8923736945309220511)
XLA Ops:
  0.6 62.7 %shard_map.50 = (f32[8,32,128]{2,1,0:T(8,128)}, f32[8,32,128]{2,1,0:T(8,128)}) custom-call(f32[8,2,2,128,128]{4,3,2,1,0:T(8,128)} %bitcast.2, f32[8,128,128]{2,1,0:T(8,128)} %u_hbm.1, f32[8,2,2,128,128]{4,3,2,1,0:T(8,128)} %bitcast.3), custom_call_target="tpu_custom_call" | custom-call | tf_op jit(solution)/shard_map/pallas_call | solution.py:503
  63.3 1.6 %copy.7 = f32[8,32,128]{2,1,0:T(8,128)} copy(f32[8,32,128]{2,1,0:T(8,128)} %get-tuple-element.4) | data formatting | bytes 262144
  64.9 1.6 %copy.8 = f32[8,32,128]{2,1,0:T(8,128)} copy(f32[8,32,128]{2,1,0:T(8,128)} %get-tuple-element.5) | data formatting | bytes 262144

commit v5 on v4

--- a/solution.py
+++ b/solution.py
@@ -14,7 +14,8 @@
 S = 8
 ROWS = 32
 NX, NY = 4, 4
-EARLY = 6
+RELAY_AT = (6, 7)
+EARLY = 4
 
 
 def split(a):
@@ -77,9 +78,9 @@
 def kernel(
     g_hbm, u_hbm, c_hbm, on_ref, cp_ref,
     g, u, c, link, head, own, tbuf, xs, ys, ex, ey, lp, lo, zbuf, dbuf, zrecv, xin,
-    ap, maps, w0, q, gg, vv, xt, w,
+    ap, maps, mp, w0, q, gg, vv, xt, w,
     stage, up, down_rows, mid, kept, from_below, from_above, passed,
-    g_sem, in_sem, pair_sem, x_send, x_recv, y_send, y_recv, z_sem, d_sem, h_sem,
+    g_sem, u_sem, in_sem, pair_sem, x_send, x_recv, y_send, y_recv, z_sem, d_sem, h_sem,
     r_send, r_recv, p_send, p_recv,
 ):
     s = lax.axis_index("slab")
@@ -115,11 +116,12 @@
     def g_copy(i):
         return pltpu.make_async_copy(g_hbm.at[i], g.at[i], g_sem.at[i])
 
-    cu = pltpu.make_async_copy(u_hbm, u, in_sem.at[0])
-    cc = pltpu.make_async_copy(c_hbm, c, in_sem.at[1])
-    g_copy(S - 1).start()
-    cu.start()
-    for i in range(S - 2, -1, -1):
+    def u_copy(i):
+        return pltpu.make_async_copy(u_hbm.at[i], u.at[i], u_sem.at[i])
+
+    cc = pltpu.make_async_copy(c_hbm, c, in_sem)
+    for i in range(S - 1, -1, -1):
+        u_copy(i).start()
         g_copy(i).start()
     cc.start()
 
@@ -132,18 +134,18 @@
     def cat(ref, i, k):
         return jnp.concatenate([ref[i, k, 0], ref[i, k, 1]], 1)
 
-    cu.wait()
-    g_copy(S - 1).wait()
+    u_copy(S - 1).wait()
     last_u = u[S - 1] * jnp.where(last, 0.0, 1.0).astype(F32)
     for k in range(2):
         ap[S - 1, k, 1] = jnp.concatenate([last_u, jnp.zeros((B, B), F32)], 1)
 
     def make_link(i):
+        u_copy(i).wait()
+        g_copy(i + 1).wait()
         uu = lhs(u[i])
         for k in range(2):
             gh, gl = split(jnp.concatenate([g[i + 1, k, 0], g[i + 1, k, 1]], 0))
             link[i, k] = mul(uu, (gh, gl), True)
-        g_copy(i).wait()
 
     make_link(S - 2)
     make_link(S - 3)
@@ -152,6 +154,7 @@
             ap[i, k, 1] = mul(lhs(link[i, k]), rhs(ap[i + 1, k, 1]))
         if i > 1:
             make_link(i - 2)
+    g_copy(0).wait()
     for k in range(2):
         head[k] = jnp.concatenate([g[0, k, 0].T, g[0, k, 1].T], 1)
         own[k, 1] = mul(lhs(head[k]), rhs(ap[0, k, 1]))
@@ -315,6 +318,14 @@
     maps[1, 0] = o
     maps[1, 1] = p
     yo.forward()
+    ey[0, 1] = prod(ys[1, 1], lp[1, 1])
+    ey[1, 1] = lp[1, 1]
+    ey[2, 1] = ys[3, 1]
+    ey[3, 1] = unit
+    ly = [lhs(maps[n, 1]) for n in range(2)]
+    ry = rhs(ey[y, 1])
+    for n in range(2):
+        mp[n] = mul(ly[n], ry)
     for i in range(4, EARLY):
         prepare(i)
     yo.finish()
@@ -324,17 +335,14 @@
     def _():
         zcopy.start()
 
-    later(ys, ey, 1)
-    outer_y = (ey[y, 0], ey[y, 1])
-    ly = [lhs(maps[n, 1]) for n in range(2)]
-    half = [mul(ly[n], rhs(ey[y, 0])) for n in range(2)]
-    prods = [mul(ly[n], rhs(ey[y, 1])) for n in range(2)]
-    offs = [
-        maps[n, 0] + mul(lhs(half[n]), rhs_t(maps[n, 1]), True) for n in range(2)
-    ]
+    ey[0, 0] = apply_map(ys[1, 0], ys[1, 1], lo[1])
+    ey[1, 0] = lo[1]
+    ey[2, 0] = ys[3, 0]
+    ey[3, 0] = zero
+    ry = rhs(ey[y, 0])
+    half = [mul(lhs(maps[n, 1]), ry) for n in range(2)]
     for n in range(2):
-        maps[n, 0] = offs[n]
-        maps[n, 1] = prods[n]
+        maps[n, 0] += mul(lhs(half[n]), rhs_t(maps[n, 1]), True)
 
     give, keep = core, 1 - core
 
@@ -347,14 +355,14 @@
     def _():
         prepare(EARLY)
         zcopy.wait_recv()
-        dbuf[...] = apply_map(maps[give, 0], maps[give, 1], zrecv[...])
+        dbuf[...] = apply_map(maps[give, 0], mp[give], zrecv[...])
 
     down = remote(dbuf, xin.at[core], d_sem.at[0], d_sem.at[1], (partner, e))
     down.start()
 
     @pl.when(z == 0)
     def _():
-        xin[core] = apply_map(maps[keep, 0], maps[keep, 1], zrecv[...])
+        xin[core] = apply_map(maps[keep, 0], mp[keep], zrecv[...])
 
     def weigh(i, k):
         zk = mul(q[i, k], (xt[k, 0], xt[k, 1]))
@@ -380,7 +388,6 @@
     def _():
         halo.start()
 
-    ready = EARLY + 1 - z
 
     def spread(i, n):
         return remote(
@@ -409,21 +416,22 @@
             pass_on(pair_no, kind).start()
         return carry
 
-    def finals(i, carry):
+    def finals(i):
         stage[0] = w[i, 0, :, 0:B] + w[i, 1, :, 0:B]
-
-        @pl.when((i < S - 1) & (i + 1 >= ready))
-        def _():
+        if i + 1 == EARLY:
+
+            @pl.when(z == 1)
+            def _():
+                prepare(EARLY)
+
+        elif EARLY < i + 1 < S:
             prepare(i + 1)
-
-        @pl.when(i < S - 1)
-        def _():
+        if i < S - 1:
             zs = [mul(q[i + 1, k], (xt[k, 0], xt[k, 1])) for k in range(2)]
             for k in range(2):
                 w[i + 1, k] = w0[i + 1, k] + mul(lhs(zs[k]), rhs_t(gg[i + 1, k]), True)
-
-        @pl.when(i == S - 1)
-        def _():
+        else:
+
             @pl.when(s < slabs - 1)
             def _():
                 halo.wait_recv()
@@ -453,10 +461,12 @@
         mid[1, i] = rows_of(1, 1)
         for kind in range(2):
             kept[i, kind] = rows_of(kind, 0)
-        return carry
-
-    lax.fori_loop(0, S, finals, 0)
-    lax.fori_loop(0, S // 2, pass_step, 0)
+
+    for i in range(S):
+        finals(i)
+        if i in RELAY_AT:
+            pass_step(RELAY_AT.index(i), 0)
+    lax.fori_loop(len(RELAY_AT), S // 2, pass_step, 0)
 
     def collect(pair_no, carry):
         for kind in range(2):
@@ -525,6 +535,7 @@
             vmem((2,) + block, F32),
             vmem((S, 2, 2) + block, F32),
             vmem((2, 2) + block, F32),
+            vmem((2,) + block, F32),
             vmem((S, 2) + block, F32),
             vmem((S, 2, 2 * B, 2 * B), BF16),
             vmem((S, 2) + block, F32),
@@ -540,7 +551,8 @@
             vmem((S, 2, ROWS, B), F32),
             vmem((2, S, ROWS, B), F32),
             dma((S,)),
-            dma((2,)),
+            dma((S,)),
+            dma,
             dma((2, 2)),
             dma((2, 6)),
             dma((2, 6)),

time: 66.6 us -> 66.1 us (level)
  no operation moved by 1% of the time
where the time goes in v5:
time: 66.1 us; the launch traced here: 65.9 us
  Pallas kernels  62.2 us (94%)
  local copies, waits for them, and re-layouts  3.14 us (5%)
    pallas_call x1, Pallas kernels, on_device(): pl.pallas_call(kernel, out_shape=(out, out), in_specs=[pl.BlockSpec(memor...  62.2 us
    unnamed x2, local copies, waits for them, and re-layouts  3.14 us

profile of v5, /device:TPU:1, one launch (start us, length us, event | category | flops | bytes accessed | tf_op | source)
XLA Modules:
  0.0 65.9 jit_solution(2672804318107744070)
XLA Ops:
  0.6 62.2 %shard_map.50 = (f32[8,32,128]{2,1,0:T(8,128)}, f32[8,32,128]{2,1,0:T(8,128)}) custom-call(f32[8,2,2,128,128]{4,3,2,1,0:T(8,128)} %bitcast.2, f32[8,128,128]{2,1,0:T(8,128)} %u_hbm.1, f32[8,2,2,128,128]{4,3,2,1,0:T(8,128)} %bitcast.3), custom_call_target="tpu_custom_call" | custom-call | tf_op jit(solution)/shard_map/pallas_call | solution.py:513
  62.8 1.6 %copy.7 = f32[8,32,128]{2,1,0:T(8,128)} copy(f32[8,32,128]{2,1,0:T(8,128)} %get-tuple-element.4) | data formatting | bytes 262144
  64.4 1.6 %copy.8 = f32[8,32,128]{2,1,0:T(8,128)} copy(f32[8,32,128]{2,1,0:T(8,128)} %get-tuple-element.5) | data formatting | bytes 262144

commit v6 on v5

--- a/solution.py
+++ b/solution.py
@@ -15,7 +15,7 @@
 ROWS = 32
 NX, NY = 4, 4
 RELAY_AT = (6, 7)
-EARLY = 4
+EARLY = 5
 
 
 def split(a):
@@ -317,6 +317,8 @@
     maps[0, 1] = ex[x, 1]
     maps[1, 0] = o
     maps[1, 1] = p
+    for i in range(4, EARLY):
+        prepare(i)
     yo.forward()
     ey[0, 1] = prod(ys[1, 1], lp[1, 1])
     ey[1, 1] = lp[1, 1]
@@ -326,8 +328,6 @@
     ry = rhs(ey[y, 1])
     for n in range(2):
         mp[n] = mul(ly[n], ry)
-    for i in range(4, EARLY):
-        prepare(i)
     yo.finish()
     zbuf[...] = level_o(ys, 1)
 

time: 66.1 us -> 67.5 us (1.021)
  Pallas kernels: 62.2 us -> 63.6 us
    pallas_call x1, Pallas kernels: 62.2 us -> 63.6 us  [on_device(): pl.pallas_call(kernel, out_shape=(out, out), in_specs=[pl.BlockSpec(memor...]
where the time goes in v6:
time: 67.5 us; the launch traced here: 67.3 us
  Pallas kernels  63.6 us (94%)
  local copies, waits for them, and re-layouts  3.14 us (5%)
    pallas_call x1, Pallas kernels, on_device(): pl.pallas_call(kernel, out_shape=(out, out), in_specs=[pl.BlockSpec(memor...  63.6 us
    unnamed x2, local copies, waits for them, and re-layouts  3.14 us

profile of v6, /device:TPU:1, one launch (start us, length us, event | category | flops | bytes accessed | tf_op | source)
XLA Modules:
  0.0 67.3 jit_solution(16877084152181287723)
XLA Ops:
  0.6 63.6 %shard_map.50 = (f32[8,32,128]{2,1,0:T(8,128)}, f32[8,32,128]{2,1,0:T(8,128)}) custom-call(f32[8,2,2,128,128]{4,3,2,1,0:T(8,128)} %bitcast.2, f32[8,128,128]{2,1,0:T(8,128)} %u_hbm.1, f32[8,2,2,128,128]{4,3,2,1,0:T(8,128)} %bitcast.3), custom_call_target="tpu_custom_call" | custom-call | tf_op jit(solution)/shard_map/pallas_call | solution.py:513
  64.2 1.6 %copy.7 = f32[8,32,128]{2,1,0:T(8,128)} copy(f32[8,32,128]{2,1,0:T(8,128)} %get-tuple-element.4) | data formatting | bytes 262144
  65.8 1.6 %copy.8 = f32[8,32,128]{2,1,0:T(8,128)} copy(f32[8,32,128]{2,1,0:T(8,128)} %get-tuple-element.5) | data formatting | bytes 262144
